TPU v7x, 256 devices: a whole 4x4x8 slice. The times are simulated.
256 devices in a mesh: dp: 16 (over z, core), tensor: 16 (over y, x).
Axes of the slice: x: 4, y: 4, z: 8, core: 2. Of those that a mesh axis runs over, the one named last changes fastest.
Arguments:
- out_grad: bfloat16 [16384, 4096], P('dp'), may hold values from -6 to 6
- gate_pre: bfloat16 [16384, 11008], P('dp', 'tensor'), may hold values from -6 to 6
- up_pre: bfloat16 [16384, 11008], P('dp', 'tensor'), may hold values from -6 to 6
- down_weight: bfloat16 [11008, 4096], P('tensor'), may hold values from -0.09375 to 0.09375
- proj_hidden: bfloat16 [11008, 64], P('tensor'), may hold values from -0.0546875 to 0.0546875
- proj_out: bfloat16 [4096, 64], replicated, may hold values from -0.09375 to 0.09375
- example_ids: int32 [16384], P('dp'), may hold values from 0 to 63, never falling along the last dimension, each value on 1 to 512 neighbouring positions
- queries: bfloat16 [4096, 4096], P('dp', 'tensor'), may hold values from -0.01171875 to 0.01171875
Outputs:
- gate_grad: bfloat16 [16384, 11008], P('dp', 'tensor')
- up_grad: bfloat16 [16384, 11008], P('dp', 'tensor')
- scores: float32 [64, 4096], P('tensor', 'dp')
Inputs may be any that keep to these rules, and one draw needn't show every extreme that they name: `example_ids`: example numbers never fall along the tokens; each example holds 1 to 512 tokens and one holds exactly that many.
All inputs are finite; a program needn't handle non-finite values.
Results may differ from a plain program's by a relative error of at most 0.0049.
Values may be sent and summed in bfloat16 or wider, within the bound.
No kernel may reach another device: no remote copies, remote signals or barrier semaphores. Data moves between devices by JAX's collectives and lax.ppermute only.
A program may use at most 64 MiB of HBM per device.

v0:
```python
import jax
import jax.numpy as jnp
from jax import lax
from jax.sharding import PartitionSpec as P

EX_DEV = 4


def on_device(out_grad, gate_pre, up_pre, down_weight, proj_hidden, proj_out, example_ids, queries):
    gate_val = gate_pre.astype(jnp.float32)
    up_val = up_pre.astype(jnp.float32)
    sigmoid_gate = jax.nn.sigmoid(gate_val)
    hidden = (gate_val * sigmoid_gate * up_val).astype(jnp.bfloat16)
    act_part = jnp.dot(hidden, proj_hidden, preferred_element_type=jnp.float32)
    rank_count = proj_hidden.shape[1]
    local_ranks = rank_count // lax.axis_size("tensor")
    rank_start = lax.axis_index("tensor") * local_ranks
    grad_proj = jnp.dot(out_grad, proj_out, preferred_element_type=jnp.float32)
    act_proj = lax.psum(act_part, "tensor")
    act_local = lax.dynamic_slice_in_dim(act_proj, rank_start, local_ranks, 1)
    hidden_grad = lax.dot_general(
        out_grad, down_weight, (((1,), (1,)), ((), ())), preferred_element_type=jnp.float32
    )
    up_grad = (hidden_grad * gate_val * sigmoid_gate).astype(jnp.bfloat16)
    gate_grad = (
        hidden_grad * up_val * sigmoid_gate * (1.0 + gate_val * (1.0 - sigmoid_gate))
    ).astype(jnp.bfloat16)
    token_count = out_grad.shape[0]
    example_count = EX_DEV * lax.axis_size("dp")
    member = (example_ids[:, None] == jnp.arange(example_count, dtype=jnp.int32)[None, :]).astype(
        jnp.float32
    )
    weighted = (member[:, :, None] * act_local[:, None, :]).reshape(
        token_count, example_count * local_ranks
    )
    partial_grads = lax.dot_general(
        weighted, grad_proj, (((0,), (0,)), ((), ())), precision=lax.Precision.HIGHEST
    )
    partial_grads = partial_grads.reshape(example_count, local_ranks * rank_count)
    summed_grads = lax.psum(partial_grads, "dp")
    example_grads = summed_grads.astype(jnp.bfloat16)
    example_block = lax.all_to_all(example_grads, "tensor", split_axis=0, concat_axis=1, tiled=True)
    score_block = lax.dot_general(
        example_block,
        lax.all_gather(queries, "tensor", axis=1, tiled=True),
        (((1,), (1,)), ((), ())),
        preferred_element_type=jnp.float32,
    )
    return (gate_grad, up_grad, score_block)


def solution(mesh):
    in_specs = (
        P("dp", None),
        P("dp", "tensor"),
        P("dp", "tensor"),
        P("tensor", None),
        P("tensor", None),
        P(),
        P("dp"),
        P("dp", "tensor"),
    )
    out_specs = (P("dp", "tensor"), P("dp", "tensor"), P("tensor", "dp"))
    return jax.shard_map(
        on_device, mesh=mesh, in_specs=in_specs, out_specs=out_specs, check_vma=False
    )
```

profile of v0, /device:TPU:2, one launch (start us, length us, event | category | flops | bytes accessed | tf_op | source)
XLA Modules:
  0.0 187.1 jit_solution(9121008205881003147)
XLA Ops:
  7.2 0.0 copy-start
  7.2 0.0 copy-start.1
  7.2 0.0 all-reduce.2.cloned.1.call-start
  7.2 3.6 %fusion.10 = f32[1024,64]{0,1:T(8,128)} fusion(bf16[688,64]{0,1:T(8,128)(2,1)} %param.12, bf16[1024,688]{0,1:T(8,128)(2,1)} %param.10, bf16[1024,688]{0,1:T(8,128)(2,1)} %param.9), kind=kOutput, calls=%fused_computation.16 | convolution fusion | flops 95813632 | bytes 3168256 | tf_op jit(solution)/shard_map/dot_general | solution.py:14
  10.8 0.0 all-reduce.2.cloned.1.call-update
  10.8 0.0 all-gather.2.cloned.1.call-start
  10.9 0.7 all-gather.2.cloned.1.call-update
  11.6 0.0 copy-done.1
  11.6 0.0 copy-done
  11.6 5.7 %fusion.14 = f32[1024,64]{1,0:T(8,128)S(1)} fusion(bf16[1024,4096]{1,0:T(8,128)(2,1)} %param.8, bf16[4096,64]{0,1:T(8,128)(2,1)S(1)} %copy-done), kind=kOutput, calls=%fused_computation.22 | convolution fusion | flops 536870912 | bytes 9175040 | tf_op jit(solution)/shard_map/dot_general | solution.py:18
  17.3 91.4 %all-reduce.2.cloned.1.call-done = f32[1024,64]{0,1:T(8,128)} async-done(((f32[1024,64]{0,1:T(8,128)}), f32[1024,64]{0,1:T(8,128)}) %all-reduce.2.cloned.1.call-update) | async-done | bytes 262160 | tf_op jit(solution)/shard_map/psum | solution.py:19
  108.8 0.8 constant_dynamic-slice_fusion
  109.5 0.3 broadcast_multiply_fusion
  109.8 0.4 mul.56
  110.2 1.0 fusion.15
  111.2 0.1 reshape.39
  111.3 46.6 %psum.15 = bf16[64,256]{1,0:T(8,128)(2,1)S(1)} all-reduce(f32[64,256]{1,0:T(8,128)S(1)} %reshape.39), channel_id=1, replica_groups=mesh['dp'=16,'tensor'=16] {'dp'}, use_global_device_ids=true, to_apply=%region_1.0 | all-reduce | flops 16384 | bytes 98304 | tf_op jit(solution)/shard_map/psum | solution.py:40
  157.9 0.6 all_to_all.14
  158.5 5.8 %all-to-all-start = ((bf16[16,4,256]{2,1,0:T(4,128)(2,1)}), bf16[16,4,256]{2,1,0:T(4,128)(2,1)S(1)}, u32[]{:S(2)}, u32[]{:S(2)}) async-start(bf16[16,4,256]{2,1,0:T(4,128)(2,1)} %all_to_all.14), calls=%async_computation | async-start | bytes 65536 | tf_op jit(solution)/shard_map/all_to_all | solution.py:42
  164.3 13.1 %fusion.9 = (bf16[1024,688]{0,1:T(8,128)(2,1)}, bf16[1024,688]{0,1:T(8,128)(2,1)}) fusion(bf16[1024,688]{0,1:T(8,128)(2,1)} %param.9, bf16[1024,688]{0,1:T(8,128)(2,1)} %param.10, bf16[1024,4096]{1,0:T(8,128)(2,1)} %param.8, bf16[688,4096]{1,0:T(8,128)(2,1)} %param.11), kind=kOutput, calls=%fused_computation.15 | convolution fusion | flops 5781929984 | bytes 19660800 | tf_op jit(solution)/shard_map/dot_general | solution.py:21
  177.4 0.0 all-to-all-done
  177.4 0.0 all-gather.2.cloned.1.call-done
  177.4 2.8 %fusion.16 = f32[4,256]{1,0:T(4,128)} fusion(bf16[4,4096]{1,0:T(4,128)(2,1)S(1)} %bitcast.14, bf16[256,4096]{1,0:T(8,128)(2,1)} %all-gather.2.cloned.1.call-done), kind=kOutput, calls=%fused_computation.24 | convolution fusion | flops 8388608 | bytes 2134016 | tf_op jit(solution)/shard_map/dot_general | solution.py:43
  (1 shorter events, 0.0 us)
Async XLA Ops:
  7.2 4.4 %copy-start = (bf16[4096,64]{0,1:T(8,128)(2,1)S(1)}, bf16[4096,64]{0,1:T(8,128)(2,1)}, u32[]{:S(2)}) copy-start(bf16[4096,64]{0,1:T(8,128)(2,1)} %param.13) | copy-start | bytes 1572868
  7.2 4.4 %copy-start.1 = (s32[1024]{0:T(1024)S(1)}, s32[1024]{0:T(1024)}, u32[]{:S(2)}) copy-start(s32[1024]{0:T(1024)} %param.14) | copy-start | bytes 12292
  7.2 101.6 %all-reduce.2.cloned.1.call-start = ((), (), s32[]{:S(2)}) async-start(), calls=%async_computation.1 | async-start | bytes 524288 | tf_op jit(solution)/shard_map/psum | solution.py:19
  10.8 166.6 %all-gather.2.cloned.1.call-start = ((), (), s32[]{:S(2)}) async-start(), calls=%async_computation.2 | async-start | bytes 2228224 | tf_op jit(solution)/shard_map/all_gather | solution.py:45
  158.5 18.9 %all-to-all-start = ((bf16[16,4,256]{2,1,0:T(4,128)(2,1)}), bf16[16,4,256]{2,1,0:T(4,128)(2,1)S(1)}, u32[]{:S(2)}, u32[]{:S(2)}) async-start(bf16[16,4,256]{2,1,0:T(4,128)(2,1)} %all_to_all.14), calls=%async_computation | async-start | bytes 65536 | tf_op jit(solution)/shard_map/all_to_all | solution.py:42
Sparse Core Ops, SparseCore 0:
  11.8 96.9 all-reduce.1
  111.5 52.3 all-gather.1
where the time goes:
time: 187 us
  waiting for transfers between devices  92.2 us (49%)
  blocking collectives  46.6 us (25%)
  matrix products  26.2 us (14%)
  between operations  14.1 us (8%)
  starting transfers between devices  5.87 us (3%)
    psum x1, waiting for transfers between devices, on_device(): act_proj = lax.psum(act_part, 'tensor')  91.4 us
    psum x1, blocking collectives, on_device(): summed_grads = lax.psum(partial_grads, 'dp')  46.6 us
    dot_general x1, matrix products, on_device(): lax.dot_general(out_grad, down_weight, (((1,), (1,)), ((), ())), preferre...  13.1 us
    all_to_all x1, starting transfers between devices, on_device(): lax.all_to_all(example_grads, 'tensor', split_axis=0, concat_axis=1, tile...  5.79 us
    dot_general x1, matrix products, on_device(): grad_proj = jnp.dot(out_grad, proj_out, preferred_element_type=jnp.float32)  5.7 us
  transfers between devices with their start and end apart: 3, of which 1 were waited for; matrix products, arithmetic and copies ran while one was open for 11% of the time, Pallas kernels for 0%

commit v1 on v0

v1 whole, which is shorter than its diff:
```python
import functools
import jax
import jax.numpy as jnp
from jax import lax
from jax.experimental import pallas as pl
from jax.experimental.pallas import tpu as pltpu
from jax.sharding import PartitionSpec as P

F32 = jnp.float32
BF16 = jnp.bfloat16
EXAMPLES = 64
MAX_COPIES = 80
ACT_PARTS = ((0, 256), (256, 256), (512, 176))
LIMIT = 60 << 20
LAST_ROWS = ((192, 256), (448, 240))
FIRST = (
    True,
    ((0, 192),),
    (0, 1, 2, 3),
    (("grad", 1), ("grad", 2), ("value", 0), ("grad", 3)),
    (
        ((("grad", 1),), ((0, 1),), ()),
        ((("grad", 2), ("value", 0)), ((0, 2),), ()),
        ((("grad", 3),), ((0, 3),), (0,)),
    ),
)
SECOND = (
    False,
    LAST_ROWS,
    (0, 1, 2),
    (("grad", 1), ("weight", 1), ("value", 0), ("value", 1), ("grad", 2)),
    (
        ((("grad", 1),), ((0, 1),), ()),
        ((("weight", 1), ("value", 0)), ((1, 0), (1, 1)), ()),
        ((("value", 1), ("grad", 2)), ((0, 2), (1, 2)), (0, 1)),
    ),
)
THIRD = (
    False,
    LAST_ROWS,
    (3,),
    (("weight", 1), ("value", 0), ("value", 1)),
    (((("weight", 1), ("value", 0), ("value", 1)), ((1, 3),), (0, 1)),),
)
TOK_BLOCK = 256
NT = (((1,), (1,)), ((), ()))
HBM = pl.BlockSpec(memory_space=pltpu.HBM)
ANY = pl.BlockSpec(memory_space=pl.ANY)
VMEM = pl.BlockSpec(memory_space=pltpu.VMEM)
MIB = 1 << 20


def act_kernel(gate_ref, up_ref, proj_ref, out_ref, gates, ups, projs, sems):
    proj_copy = pltpu.make_async_copy(proj_ref, projs, sems.at[0])
    copies = []
    for index, (start, rows) in enumerate(ACT_PARTS):
        part = pl.ds(start, rows)
        copies.append((
            pltpu.make_async_copy(gate_ref.at[part], gates.at[part], sems.at[1 + 2 * index]),
            pltpu.make_async_copy(up_ref.at[part], ups.at[part], sems.at[2 + 2 * index]),
        ))
    for gate_copy, up_copy in copies[:1]:
        gate_copy.start()
        up_copy.start()
    proj_copy.start()
    for gate_copy, up_copy in copies[1:]:
        gate_copy.start()
        up_copy.start()
    act = None
    for (gate_copy, up_copy), (start, rows) in zip(copies, ACT_PARTS):
        gate_copy.wait()
        up_copy.wait()
        gate = gates[start:start + rows, :].astype(F32)
        up = ups[start:start + rows, :].astype(F32)
        hidden = (gate * jax.nn.sigmoid(gate) * up).astype(BF16)
        if act is None:
            proj_copy.wait()
        term = jnp.dot(projs[:, start:start + rows], hidden, preferred_element_type=F32)
        act = term if act is None else act + term
    for part in range(16):
        for block in range(8):
            out_ref[part, 4 * block:4 * block + 4, :] = act[
                4 * part:4 * part + 4, 128 * block:128 * block + 128
            ]


def act_parts(gate, up, proj):
    hidden_units, tokens = gate.shape
    ranks = proj.shape[0]
    return pl.pallas_call(
        act_kernel,
        in_specs=[HBM] * 3,
        out_specs=VMEM,
        out_shape=jax.ShapeDtypeStruct((16, 32, 128), F32),
        scratch_shapes=[
            pltpu.VMEM(gate.shape, BF16),
            pltpu.VMEM(gate.shape, BF16),
            pltpu.VMEM(proj.shape, BF16),
            pltpu.SemaphoreType.DMA((1 + 2 * len(ACT_PARTS),)),
        ],
        compiler_params=pltpu.CompilerParams(vmem_limit_bytes=LIMIT),
        cost_estimate=pl.CostEstimate(
            flops=2 * ranks * hidden_units * tokens,
            bytes_accessed=4 * hidden_units * tokens,
            transcendentals=hidden_units * tokens,
        ),
        name="act_parts",
    )(gate, up, proj)


def grads_kernel(plan, grad_ref, weight_ref, gate_ref, up_ref, *rest):
    first, row_parts, tok_parts, loads, blocks = plan
    if first:
        proj_ref, gate_out, up_out, order_out, proj_out = rest[:5]
        rank = proj_ref.shape[0]
    else:
        gate_out, up_out, order_out = rest[3:6]
        rank = 0
    grads, weights, gates, ups, gate_done, up_done, products, sems = rest[-8:]
    width = grads.shape[1]
    first_row, first_tok = row_parts[0][0], tok_parts[0]
    all_tokens = pl.ds(TOK_BLOCK * first_tok, TOK_BLOCK * len(tok_parts))
    sem = iter(range(MAX_COPIES))
    copies = {}

    def start(key, *pairs):
        for source, target in pairs:
            part = pltpu.make_async_copy(source, target, sems.at[next(sem)])
            part.start()
            copies.setdefault(key, []).append(part)

    def wait(*keys):
        for key in keys:
            for part in copies.pop(key):
                part.wait()

    def tokens(part):
        return pl.ds(TOK_BLOCK * part, TOK_BLOCK)

    def local_tokens(part):
        return pl.ds(TOK_BLOCK * (part - first_tok), TOK_BLOCK)

    def rows(part):
        return pl.ds(*row_parts[part])

    def local_rows(part):
        row, size = row_parts[part]
        return pl.ds(row - first_row, size)

    def load(kind, part, half=None):
        columns = pl.ds(0, width) if half is None else pl.ds(width // 2 * half, width // 2)
        key = (kind, part) if half is None else (kind, part, half)
        if kind == "grad":
            target = grads.at[local_tokens(part), columns]
            start(key, (grad_ref.at[tokens(part), columns], target))
        elif kind == "weight":
            row, size = row_parts[part]
            target = weights.at[pl.ds(rank + row - first_row, size), columns]
            start(key, (weight_ref.at[rows(part), columns], target))
        elif kind == "proj":
            start(key, (proj_ref.at[:, columns], weights.at[pl.ds(0, rank), columns]))
        else:
            place = (rows(part), all_tokens)
            start(
                key,
                (gate_ref.at[place], gates.at[local_rows(part), :]),
                (up_ref.at[place], ups.at[local_rows(part), :]),
            )

    def multiply(row_part, tok_part, columns):
        row, size = row_parts[row_part]
        area = pl.ds(rank + row - first_row, size) if row_part else pl.ds(0, rank + size)
        return lax.dot_general(
            weights[area, columns],
            grads[local_tokens(tok_part), columns],
            NT,
            preferred_element_type=F32,
        )

    def keep(row_part, tok_part, product):
        tok = local_tokens(tok_part)
        if first and row_part == 0:
            projected = product[:rank]
            high = projected.astype(BF16)
            proj_out[:rank, tok] = high
            proj_out[rank:, tok] = (projected - high.astype(F32)).astype(BF16)
            product = product[rank:]
        products[local_rows(row_part), tok] = product

    def finish(row_part, tok_part):
        here = (local_rows(row_part), local_tokens(tok_part))
        gate = gates[here].astype(F32)
        sig = jax.nn.sigmoid(gate)
        scaled = products[here] * sig
        up_done[here] = (scaled * gate).astype(BF16)
        gate_done[here] = (
            scaled * ups[here].astype(F32) * (1.0 + gate * (1.0 - sig))
        ).astype(BF16)

    def store(row_part):
        place = (rows(row_part), all_tokens)
        here = local_rows(row_part)
        start(
            "out",
            (gate_done.at[here, :], gate_out.at[place]),
            (up_done.at[here, :], up_out.at[place]),
        )

    kinds = [("grad", first_tok), ("weight", 0)] + [("proj", 0)] * first
    for half in range(2):
        for kind, part in kinds:
            load(kind, part, half)
    for kind, part in loads:
        load(kind, part)
    product = None
    for half in range(2):
        wait(*((*key, half) for key in kinds))
        term = multiply(0, first_tok, pl.ds(width // 2 * half, width // 2))
        product = term if product is None else product + term
    keep(0, first_tok, product)
    pending = [(0, first_tok)]
    for needs, tiles, rows_done in blocks:
        wait(*needs)
        for tile in tiles:
            keep(*tile, multiply(*tile, slice(None)))
            pending.append(tile)
            while len(pending) > 1 and ("value", pending[0][0]) not in copies:
                finish(*pending.pop(0))
        if rows_done:
            while pending:
                finish(*pending.pop(0))
        for row_part in rows_done:
            store(row_part)
    wait("out")


def grads_call(plan, grad, weight, gate, up, proj=None, before=None, after=None):
    first, row_parts, tok_parts = plan[:3]
    width = grad.shape[1]
    rows = sum(size for _, size in row_parts)
    tokens = TOK_BLOCK * len(tok_parts)
    in_specs = [HBM] * 4
    out_specs = [HBM, HBM, HBM]
    out_shape = [jax.ShapeDtypeStruct(gate.shape, BF16)] * 2 + [jax.ShapeDtypeStruct((8, 128), F32)]
    if first:
        in_specs.append(HBM)
        out_specs.append(VMEM)
        out_shape.append(jax.ShapeDtypeStruct((2 * proj.shape[0], tokens), BF16))
        extra, aliases = (proj,), {}
    else:
        in_specs += [HBM, HBM, ANY]
        extra, aliases = (*before, after), {4: 0, 5: 1}
    return pl.pallas_call(
        functools.partial(grads_kernel, plan),
        in_specs=in_specs,
        out_specs=out_specs,
        out_shape=out_shape,
        scratch_shapes=[
            pltpu.VMEM((tokens, width), BF16),
            pltpu.VMEM((rows + 64 * first, width), BF16),
            *[pltpu.VMEM((rows, tokens), BF16)] * 4,
            pltpu.VMEM((rows, tokens), F32),
            pltpu.SemaphoreType.DMA((MAX_COPIES,)),
        ],
        input_output_aliases=aliases,
        compiler_params=pltpu.CompilerParams(vmem_limit_bytes=LIMIT),
        cost_estimate=pl.CostEstimate(
            flops=2 * rows * tokens * width,
            bytes_accessed=2 * (tokens + rows) * width + 8 * rows * tokens,
            transcendentals=rows * tokens,
        ),
        name="grads_%d_%d" % (row_parts[0][0], tok_parts[0]),
    )(grad, weight, gate, up, *extra)


def example_kernel(parts_ref, ids_ref, proj_ref, out_ref):
    act = parts_ref[0]
    for part in range(1, 16):
        act = act + parts_ref[part]
    example = lax.broadcasted_iota(jnp.int32, (EXAMPLES, 128), 0)
    members = [ids_ref[block:block + 1, :] == example for block in range(8)]
    projected = proj_ref[...]
    for rank in range(4):
        weighted = jnp.concatenate(
            [
                jnp.where(members[block], act[4 * block + rank:4 * block + rank + 1, :], 0.0)
                for block in range(8)
            ],
            axis=1,
        )
        high = weighted.astype(BF16)
        low = (weighted - high.astype(F32)).astype(BF16)
        first = lax.dot_general(high, projected, NT, preferred_element_type=F32)
        second = lax.dot_general(low, projected[:64], NT, preferred_element_type=F32)
        out_ref[:, 64 * rank:64 * rank + 64] = first[:, :64] + (first[:, 64:] + second)


def example_terms(parts, ids, proj):
    return pl.pallas_call(
        example_kernel,
        out_shape=jax.ShapeDtypeStruct((EXAMPLES, 256), F32),
        compiler_params=pltpu.CompilerParams(vmem_limit_bytes=16 * MIB),
        cost_estimate=pl.CostEstimate(flops=100_000_000, bytes_accessed=700_000, transcendentals=0),
        name="example_terms",
    )(parts, ids, proj)


def score_kernel(terms_ref, queries_ref, _order, out_ref):
    total = terms_ref[0].astype(F32)
    for part in range(1, 8):
        total = total + terms_ref[part].astype(F32)
    scores = lax.dot_general(
        total.astype(BF16), queries_ref[...], NT, preferred_element_type=F32
    )
    for part in range(16):
        for half in range(2):
            out_ref[part, 4 * half:4 * half + 4, :] = scores[
                4 * part:4 * part + 4, 128 * half:128 * half + 128
            ]


def score_parts(terms, queries, order):
    return pl.pallas_call(
        score_kernel,
        in_specs=[VMEM, VMEM, HBM],
        out_specs=VMEM,
        out_shape=jax.ShapeDtypeStruct((16, 8, 128), F32),
        compiler_params=pltpu.CompilerParams(vmem_limit_bytes=16 * MIB),
        cost_estimate=pl.CostEstimate(flops=10_000_000, bytes_accessed=500_000, transcendentals=0),
        name="score_parts",
    )(terms, queries, order)


def final_kernel(parts_ref, _order, out_ref):
    total = parts_ref[0]
    for part in range(1, 16):
        total = total + parts_ref[part]
    out_ref[:, :128] = total[:4]
    out_ref[:, 128:] = total[4:]


def final_sum(parts, order):
    return pl.pallas_call(
        final_kernel,
        in_specs=[VMEM, HBM],
        out_specs=VMEM,
        out_shape=jax.ShapeDtypeStruct((4, 256), F32),
        compiler_params=pltpu.CompilerParams(vmem_limit_bytes=16 * MIB),
        cost_estimate=pl.CostEstimate(flops=100_000, bytes_accessed=70_000, transcendentals=0),
        name="final_sum",
    )(parts, order)


def on_device(out_grad, gate_pre, up_pre, down_weight, proj_hidden, proj_out, example_ids, queries):
    gate, up = gate_pre.T, up_pre.T
    exchange = functools.partial(
        lax.all_to_all, axis_name="tensor", split_axis=0, concat_axis=0, tiled=True
    )
    sent = act_parts(gate, up, proj_hidden.T)
    parts = exchange(sent)
    gate_grad, up_grad, _, projected = grads_call(
        FIRST, out_grad, down_weight, gate, up, proj=proj_out.T
    )
    terms = example_terms(parts, example_ids.reshape(8, 128), projected)
    other = lax.ppermute(terms, "dp", [(i, i ^ 1) for i in range(16)])
    pair = (terms + other).astype(BF16)
    pairs = jnp.broadcast_to(pair[None], (8, *pair.shape))
    chips = [[2 * z + core for z in range(8)] for core in range(2)]
    all_terms = lax.all_to_all(
        pairs, "dp", split_axis=0, concat_axis=0, tiled=True, axis_index_groups=chips
    )
    gate_grad, up_grad, order = grads_call(
        SECOND, out_grad, down_weight, gate, up, before=(gate_grad, up_grad), after=pair
    )
    scores = score_parts(all_terms, queries, order)
    score_terms = exchange(scores)
    gate_grad, up_grad, order = grads_call(
        THIRD, out_grad, down_weight, gate, up, before=(gate_grad, up_grad), after=scores
    )
    return gate_grad.T, up_grad.T, final_sum(score_terms, order)


def solution(mesh):
    in_specs = (
        P("dp", None),
        P("dp", "tensor"),
        P("dp", "tensor"),
        P("tensor", None),
        P("tensor", None),
        P(),
        P("dp"),
        P("dp", "tensor"),
    )
    out_specs = (P("dp", "tensor"), P("dp", "tensor"), P("tensor", "dp"))
    return jax.shard_map(
        on_device, mesh=mesh, in_specs=in_specs, out_specs=out_specs, check_vma=False
    )
```

time: 187 us -> 62.4 us (0.33)
  the two profiles are of different devices: /device:TPU:2 before, /device:TPU:32 now
where the time goes in v1:
time: 62.4 us; the launch traced here: 61.5 us
  Pallas kernels  31.4 us (50%)
  starting transfers between devices  22.9 us (37%)
  waiting for transfers between devices  3.34 us (5%)
  local copies, waits for them, and re-layouts  3.05 us (5%)
  between operations  0.74 us (1%)
    pallas_call x3, Pallas kernels, grads_call(): pl.pallas_call(functools.partial(grads_kernel, plan), in_specs=in_specs,...  26.2 us
    all_to_all x1, starting transfers between devices, on_device(): lax.all_to_all(pairs, 'dp', split_axis=0, concat_axis=0, tiled=True, axis...  8.57 us
    all_to_all x1, starting transfers between devices, on_device(): score_terms = exchange(scores)  7.22 us
    all_to_all x1, starting transfers between devices, on_device(): parts = exchange(sent)  7.05 us
    pallas_call x1, Pallas kernels, act_parts(): pl.pallas_call(act_kernel, in_specs=[HBM] * 3, out_specs=VMEM, out_shape=...  3.02 us
    unnamed x12, local copies, waits for them, and re-layouts  2.33 us
    all_to_all x1, waiting for transfers between devices, on_device(): score_terms = exchange(scores)  1.29 us
  transfers between devices with their start and end apart: 4, of which 3 were waited for; matrix products, arithmetic and copies ran while one was open for 0% of the time, Pallas kernels for 43%

profile of v1, /device:TPU:32, one launch (start us, length us, event | category | flops | bytes accessed | tf_op | source)
XLA Modules:
  0.0 61.5 jit_solution(2694872402637374164)
XLA Ops:
  0.6 3.0 %act_parts.1 = f32[16,32,128]{2,1,0:T(8,128)} custom-call(bf16[688,1024]{1,0:T(8,128)(2,1)} %bitcast.8, bf16[688,1024]{1,0:T(8,128)(2,1)} %bitcast.12, bf16[64,688]{1,0:T(8,128)(2,1)} %bitcast.19), custom_call_target="tpu_custom_call" | custom-call | flops 90177536 | bytes 2818048 | tf_op jit(solution)/shard_map/act_parts/pallas_call | solution.py:90
  3.7 7.1 %all-to-all-start = ((f32[16,32,128]{2,1,0:T(8,128)}), f32[16,32,128]{2,1,0:T(8,128)S(1)}, u32[]{:S(2)}, u32[]{:S(2)}) async-start(f32[16,32,128]{2,1,0:T(8,128)} %act_parts.1), calls=%async_computation | async-start | bytes 524288 | tf_op jit(solution)/shard_map/all_to_all | solution.py:360
  10.7 0.0 copy-start.2
  10.7 9.9 %grads_0_0.1 = (bf16[688,1024]{1,0:T(8,128)(2,1)}, bf16[688,1024]{1,0:T(8,128)(2,1)}, f32[8,128]{1,0:T(8,128)}, bf16[128,1024]{1,0:T(8,128)(2,1)}) custom-call(bf16[1024,4096]{1,0:T(8,128)(2,1)} %grad_ref.5, bf16[688,4096]{1,0:T(8,128)(2,1)} %weight_ref.5, bf16[688,1024]{1,0:T(8,128)(2,1)} %bitcast.9, bf16[688,1024]{1,0:T(8,128)(2,1)} %bitcast.13, ...), custom_call_target="tpu_custom_call" | custom-call | flops 1610612736 | bytes 11534336 | tf_op jit(solution)/shard_map/grads_0_0/pallas_call | solution.py:253
  20.6 0.0 all-to-all-done.parts_ref
  20.6 0.0 copy-done.2
  20.6 0.0 copy-start
  20.6 0.9 %copy-done = bf16[128,1024]{1,0:T(8,128)(2,1)S(1)} copy-done((bf16[128,1024]{1,0:T(8,128)(2,1)S(1)}, bf16[128,1024]{1,0:T(8,128)(2,1)}, u32[]{:S(2)}) %copy-start) | copy-done | bytes 262168
  21.6 0.8 %example_terms.1 = f32[64,256]{1,0:T(8,128)S(1)} custom-call(f32[16,32,128]{2,1,0:T(8,128)S(1)} %all-to-all-done.parts_ref, s32[8,128]{1,0:T(8,128)S(1)} %bitcast.7, bf16[128,1024]{1,0:T(8,128)(2,1)S(1)} %copy-done), custom_call_target="tpu_custom_call" | custom-call | flops 100000000 | bytes 700000 | tf_op jit(solution)/shard_map/example_terms/pallas_call | solution.py:299
  22.4 0.1 collective-permute-start
  22.5 1.2 %collective-permute-done = f32[64,256]{1,0:T(8,128)S(1)} collective-permute-done((f32[64,256]{1,0:T(8,128)S(1)}, f32[64,256]{1,0:T(8,128)S(1)}, u32[]{:S(2)}, u32[]{:S(2)}) %collective-permute-start) | collective-permute-done | bytes 65568 | tf_op jit(solution)/shard_map/ppermute | solution.py:365
  23.7 0.0 copy-start.5
  23.7 0.7 %broadcast_in_dim.2 = bf16[8,64,256]{2,1,0:T(8,128)(2,1)} broadcast(bf16[64,256]{1,0:T(8,128)(2,1)S(1)} %add_convert_fusion.rest_2_), dimensions={1,2} | broadcast | bytes 294912 | tf_op jit(solution)/shard_map/broadcast_in_dim | solution.py:367
  24.5 8.6 %all-to-all-start.1 = ((bf16[8,64,256]{2,1,0:T(8,128)(2,1)}), bf16[8,64,256]{2,1,0:T(8,128)(2,1)S(1)}, u32[]{:S(2)}, u32[]{:S(2)}) async-start(bf16[8,64,256]{2,1,0:T(8,128)(2,1)} %broadcast_in_dim.2), calls=%async_computation.1 | async-start | bytes 524288 | tf_op jit(solution)/shard_map/all_to_all | solution.py:369
  33.0 0.0 copy-done.5
  33.0 0.0 copy-start.1
  33.0 9.9 %grads_192_0.1 = (bf16[688,1024]{1,0:T(8,128)(2,1)}, bf16[688,1024]{1,0:T(8,128)(2,1)}, f32[8,128]{1,0:T(8,128)}) custom-call(bf16[1024,4096]{1,0:T(8,128)(2,1)} %grad_ref.5, bf16[688,4096]{1,0:T(8,128)(2,1)} %weight_ref.5, bf16[688,1024]{1,0:T(8,128)(2,1)} %bitcast.10, bf16[688,1024]{1,0:T(8,128)(2,1)} %bitcast.14, ...), custom_call_target="tpu_custom_call", output_to_operand_aliasing={{0}: (4, {}), {1}: (5, {})} | custom-call | flops 3120562176 | bytes 13402112 | tf_op jit(solution)/shard_map/grads_192_0/pallas_call | solution.py:253
  43.0 0.8 %all-to-all-done.1.terms_ref = bf16[8,64,256]{2,1,0:T(8,128)(2,1)S(1)} async-done(((bf16[8,64,256]{2,1,0:T(8,128)(2,1)}), bf16[8,64,256]{2,1,0:T(8,128)(2,1)S(1)}, u32[]{:S(2)}, u32[]{:S(2)}) %all-to-all-start.1) | async-done | bytes 262176 | tf_op jit(solution)/shard_map/all_to_all | solution.py:369
  43.8 0.0 copy-done.1
  43.8 0.0 copy-start.3
  43.8 0.7 %copy-done.3 = f32[8,128]{1,0:T(8,128)S(1)} copy-done((f32[8,128]{1,0:T(8,128)S(1)}, f32[8,128]{1,0:T(8,128)}, u32[]{:S(2)}) %copy-start.3) | copy-done | bytes 4120
  44.5 0.8 %score_parts.1.rest_2_ = f32[16,8,128]{2,1,0:T(8,128)} custom-call(bf16[8,64,256]{2,1,0:T(8,128)(2,1)S(1)} %all-to-all-done.1.terms_ref, bf16[256,256]{1,0:T(8,128)(2,1)S(1)} %copy-done.1, f32[8,128]{1,0:T(8,128)S(1)} %copy-done.3), custom_call_target="tpu_custom_call" | custom-call | flops 10000000 | bytes 500000 | tf_op jit(solution)/shard_map/score_parts/pallas_call | solution.py:323
  45.3 7.2 %all-to-all-start.2 = ((f32[16,8,128]{2,1,0:T(8,128)}), f32[16,8,128]{2,1,0:T(8,128)S(1)}, u32[]{:S(2)}, u32[]{:S(2)}) async-start(f32[16,8,128]{2,1,0:T(8,128)} %score_parts.1.rest_2_), calls=%async_computation.2 | async-start | bytes 131072 | tf_op jit(solution)/shard_map/all_to_all | solution.py:376
  52.5 6.4 %grads_192_3.1 = (bf16[688,1024]{1,0:T(8,128)(2,1)}, bf16[688,1024]{1,0:T(8,128)(2,1)}, f32[8,128]{1,0:T(8,128)}) custom-call(bf16[1024,4096]{1,0:T(8,128)(2,1)} %grad_ref.5, bf16[688,4096]{1,0:T(8,128)(2,1)} %weight_ref.5, bf16[688,1024]{1,0:T(8,128)(2,1)} %bitcast.11, bf16[688,1024]{1,0:T(8,128)(2,1)} %bitcast.15, ...), custom_call_target="tpu_custom_call", output_to_operand_aliasing={{0}: (4, {}), {1}: (5, {})} | custom-call | flops 1040187392 | bytes 7176192 | tf_op jit(solution)/shard_map/grads_192_3/pallas_call | solution.py:253
  58.9 1.3 %all-to-all-done.2.parts_ref = f32[16,8,128]{2,1,0:T(8,128)S(1)} async-done(((f32[16,8,128]{2,1,0:T(8,128)}), f32[16,8,128]{2,1,0:T(8,128)S(1)}, u32[]{:S(2)}, u32[]{:S(2)}) %all-to-all-start.2) | async-done | bytes 65568 | tf_op jit(solution)/shard_map/all_to_all | solution.py:376
  60.2 0.0 copy-start.4
  60.2 0.7 %copy-done.4 = f32[8,128]{1,0:T(8,128)S(1)} copy-done((f32[8,128]{1,0:T(8,128)S(1)}, f32[8,128]{1,0:T(8,128)}, u32[]{:S(2)}) %copy-start.4) | copy-done | bytes 4120
  60.8 0.6 final_sum.1
  (1 shorter events, 0.0 us)
Async XLA Ops:
  3.7 16.9 %all-to-all-start = ((f32[16,32,128]{2,1,0:T(8,128)}), f32[16,32,128]{2,1,0:T(8,128)S(1)}, u32[]{:S(2)}, u32[]{:S(2)}) async-start(f32[16,32,128]{2,1,0:T(8,128)} %act_parts.1), calls=%async_computation | async-start | bytes 524288 | tf_op jit(solution)/shard_map/all_to_all | solution.py:360
  10.7 9.9 %copy-start.2 = (s32[1024]{0:T(1024)S(1)}, s32[1024]{0:T(1024)}, u32[]{:S(2)}) copy-start(s32[1024]{0:T(1024)} %param.14) | copy-start | bytes 12292
  20.6 1.0 %copy-start = (bf16[128,1024]{1,0:T(8,128)(2,1)S(1)}, bf16[128,1024]{1,0:T(8,128)(2,1)}, u32[]{:S(2)}) copy-start(bf16[128,1024]{1,0:T(8,128)(2,1)} %get-tuple-element.14.proj_ref) | copy-start | bytes 786436
  22.4 1.3 %collective-permute-start = (f32[64,256]{1,0:T(8,128)S(1)}, f32[64,256]{1,0:T(8,128)S(1)}, u32[]{:S(2)}, u32[]{:S(2)}) collective-permute-start(f32[64,256]{1,0:T(8,128)S(1)} %example_terms.1), channel_id=1, source_target_pairs={{0,16},{16,0},{32,48},{48,32},{64,80},{80,64},{96,112},{112,96},{1... | collective-permute-start | bytes 196616 | tf_op jit(solution)/shard_map/ppermute | solution.py:365
  23.7 9.3 %copy-start.5 = (bf16[64,256]{1,0:T(8,128)(2,1)}, bf16[64,256]{1,0:T(8,128)(2,1)S(1)}, u32[]{:S(2)}) copy-start(bf16[64,256]{1,0:T(8,128)(2,1)S(1)} %add_convert_fusion.rest_2_) | copy-start | bytes 98308
  24.5 19.3 %all-to-all-start.1 = ((bf16[8,64,256]{2,1,0:T(8,128)(2,1)}), bf16[8,64,256]{2,1,0:T(8,128)(2,1)S(1)}, u32[]{:S(2)}, u32[]{:S(2)}) async-start(bf16[8,64,256]{2,1,0:T(8,128)(2,1)} %broadcast_in_dim.2), calls=%async_computation.1 | async-start | bytes 524288 | tf_op jit(solution)/shard_map/all_to_all | solution.py:369
  33.0 10.7 %copy-start.1 = (bf16[256,256]{1,0:T(8,128)(2,1)S(1)}, bf16[256,256]{1,0:T(8,128)(2,1)}, u32[]{:S(2)}) copy-start(bf16[256,256]{1,0:T(8,128)(2,1)} %queries_ref.1) | copy-start | bytes 393220
  43.8 0.7 %copy-start.3 = (f32[8,128]{1,0:T(8,128)S(1)}, f32[8,128]{1,0:T(8,128)}, u32[]{:S(2)}) copy-start(f32[8,128]{1,0:T(8,128)} %get-tuple-element.17._order) | copy-start | bytes 12292
  45.3 14.9 %all-to-all-start.2 = ((f32[16,8,128]{2,1,0:T(8,128)}), f32[16,8,128]{2,1,0:T(8,128)S(1)}, u32[]{:S(2)}, u32[]{:S(2)}) async-start(f32[16,8,128]{2,1,0:T(8,128)} %score_parts.1.rest_2_), calls=%async_computation.2 | async-start | bytes 131072 | tf_op jit(solution)/shard_map/all_to_all | solution.py:376
  60.2 0.7 %copy-start.4 = (f32[8,128]{1,0:T(8,128)S(1)}, f32[8,128]{1,0:T(8,128)}, u32[]{:S(2)}) copy-start(f32[8,128]{1,0:T(8,128)} %get-tuple-element.20._order) | copy-start | bytes 12292

commit v2 on v1

--- a/solution.py
+++ b/solution.py
@@ -17,30 +17,41 @@
     True,
     ((0, 192),),
     (0, 1, 2, 3),
-    (("grad", 1), ("grad", 2), ("value", 0), ("grad", 3)),
+    (("grad", 0), ("weight", 0), ("proj", 0), ("grad", 1), ("value", 0), ("grad", 2), ("grad", 3)),
     (
-        ((("grad", 1),), ((0, 1),), ()),
-        ((("grad", 2), ("value", 0)), ((0, 2),), ()),
-        ((("grad", 3),), ((0, 3),), (0,)),
+        ((("grad", 0), ("weight", 0), ("proj", 0), ("grad", 1)), ((0, 0), (0, 1)), ()),
+        ((("grad", 2), ("grad", 3), ("value", 0)), ((0, 2), (0, 3)), (0,)),
     ),
 )
 SECOND = (
     False,
     LAST_ROWS,
     (0, 1, 2),
-    (("grad", 1), ("weight", 1), ("value", 0), ("value", 1), ("grad", 2)),
     (
-        ((("grad", 1),), ((0, 1),), ()),
-        ((("weight", 1), ("value", 0)), ((1, 0), (1, 1)), ()),
-        ((("value", 1), ("grad", 2)), ((0, 2), (1, 2)), (0, 1)),
+        ("grad", 0), ("weight", 0), ("grad", 1), ("weight", 1), ("value", 0), ("grad", 2),
+        ("value", 1),
+    ),
+    (
+        ((("grad", 0), ("weight", 0), ("grad", 1)), ((0, 0), (0, 1)), ()),
+        (
+            (("weight", 1), ("value", 0), ("value", 1), ("grad", 2)),
+            ((1, 0), (1, 1), (0, 2), (1, 2)),
+            (0, 1),
+        ),
     ),
 )
 THIRD = (
     False,
     LAST_ROWS,
     (3,),
-    (("weight", 1), ("value", 0), ("value", 1)),
-    (((("weight", 1), ("value", 0), ("value", 1)), ((1, 3),), (0, 1)),),
+    (("grad", 3), ("weight", 0), ("weight", 1), ("value", 0), ("value", 1)),
+    (
+        (
+            (("grad", 3), ("weight", 0), ("weight", 1), ("value", 0), ("value", 1)),
+            ((0, 3), (1, 3)),
+            (0, 1),
+        ),
+    ),
 )
 TOK_BLOCK = 256
 NT = (((1,), (1,)), ((), ()))
@@ -147,18 +158,16 @@
         row, size = row_parts[part]
         return pl.ds(row - first_row, size)
 
-    def load(kind, part, half=None):
-        columns = pl.ds(0, width) if half is None else pl.ds(width // 2 * half, width // 2)
-        key = (kind, part) if half is None else (kind, part, half)
+    def load(kind, part):
+        key = (kind, part)
         if kind == "grad":
-            target = grads.at[local_tokens(part), columns]
-            start(key, (grad_ref.at[tokens(part), columns], target))
+            start(key, (grad_ref.at[tokens(part), :], grads.at[local_tokens(part), :]))
         elif kind == "weight":
             row, size = row_parts[part]
-            target = weights.at[pl.ds(rank + row - first_row, size), columns]
-            start(key, (weight_ref.at[rows(part), columns], target))
+            target = weights.at[pl.ds(rank + row - first_row, size), :]
+            start(key, (weight_ref.at[rows(part), :], target))
         elif kind == "proj":
-            start(key, (proj_ref.at[:, columns], weights.at[pl.ds(0, rank), columns]))
+            start(key, (proj_ref, weights.at[pl.ds(0, rank), :]))
         else:
             place = (rows(part), all_tokens)
             start(
@@ -167,12 +176,12 @@
                 (up_ref.at[place], ups.at[local_rows(part), :]),
             )
 
-    def multiply(row_part, tok_part, columns):
+    def multiply(row_part, tok_part):
         row, size = row_parts[row_part]
         area = pl.ds(rank + row - first_row, size) if row_part else pl.ds(0, rank + size)
         return lax.dot_general(
-            weights[area, columns],
-            grads[local_tokens(tok_part), columns],
+            weights[area, :],
+            grads[local_tokens(tok_part), :],
             NT,
             preferred_element_type=F32,
         )
@@ -206,23 +215,13 @@
             (up_done.at[here, :], up_out.at[place]),
         )
 
-    kinds = [("grad", first_tok), ("weight", 0)] + [("proj", 0)] * first
-    for half in range(2):
-        for kind, part in kinds:
-            load(kind, part, half)
     for kind, part in loads:
         load(kind, part)
-    product = None
-    for half in range(2):
-        wait(*((*key, half) for key in kinds))
-        term = multiply(0, first_tok, pl.ds(width // 2 * half, width // 2))
-        product = term if product is None else product + term
-    keep(0, first_tok, product)
-    pending = [(0, first_tok)]
+    pending = []
     for needs, tiles, rows_done in blocks:
         wait(*needs)
         for tile in tiles:
-            keep(*tile, multiply(*tile, slice(None)))
+            keep(*tile, multiply(*tile))
             pending.append(tile)
             while len(pending) > 1 and ("value", pending[0][0]) not in copies:
                 finish(*pending.pop(0))
@@ -305,7 +304,7 @@
     )(parts, ids, proj)
 
 
-def score_kernel(terms_ref, queries_ref, _order, out_ref):
+def score_kernel(terms_ref, queries_ref, out_ref):
     total = terms_ref[0].astype(F32)
     for part in range(1, 8):
         total = total + terms_ref[part].astype(F32)
@@ -319,19 +318,19 @@
             ]
 
 
-def score_parts(terms, queries, order):
+def score_parts(terms, queries):
     return pl.pallas_call(
         score_kernel,
-        in_specs=[VMEM, VMEM, HBM],
+        in_specs=[VMEM, VMEM],
         out_specs=VMEM,
         out_shape=jax.ShapeDtypeStruct((16, 8, 128), F32),
         compiler_params=pltpu.CompilerParams(vmem_limit_bytes=16 * MIB),
         cost_estimate=pl.CostEstimate(flops=10_000_000, bytes_accessed=500_000, transcendentals=0),
         name="score_parts",
-    )(terms, queries, order)
-
-
-def final_kernel(parts_ref, _order, out_ref):
+    )(terms, queries)
+
+
+def final_kernel(parts_ref, out_ref):
     total = parts_ref[0]
     for part in range(1, 16):
         total = total + parts_ref[part]
@@ -339,16 +338,16 @@
     out_ref[:, 128:] = total[4:]
 
 
-def final_sum(parts, order):
+def final_sum(parts):
     return pl.pallas_call(
         final_kernel,
-        in_specs=[VMEM, HBM],
+        in_specs=[VMEM],
         out_specs=VMEM,
         out_shape=jax.ShapeDtypeStruct((4, 256), F32),
         compiler_params=pltpu.CompilerParams(vmem_limit_bytes=16 * MIB),
         cost_estimate=pl.CostEstimate(flops=100_000, bytes_accessed=70_000, transcendentals=0),
         name="final_sum",
-    )(parts, order)
+    )(parts)
 
 
 def on_device(out_grad, gate_pre, up_pre, down_weight, proj_hidden, proj_out, example_ids, queries):
@@ -372,12 +371,12 @@
     gate_grad, up_grad, order = grads_call(
         SECOND, out_grad, down_weight, gate, up, before=(gate_grad, up_grad), after=pair
     )
-    scores = score_parts(all_terms, queries, order)
+    scores = score_parts(all_terms, queries)
     score_terms = exchange(scores)
     gate_grad, up_grad, order = grads_call(
         THIRD, out_grad, down_weight, gate, up, before=(gate_grad, up_grad), after=scores
     )
-    return gate_grad.T, up_grad.T, final_sum(score_terms, order)
+    return gate_grad.T, up_grad.T, final_sum(score_terms)
 
 
 def solution(mesh):

time: 62.4 us -> 59.2 us (0.949)
  Pallas kernels: 31.4 us -> 28.2 us
  waiting for transfers between devices: 3.34 us -> 5.36 us
  local copies, waits for them, and re-layouts: 3.05 us -> 1.68 us
    pallas_call x3, Pallas kernels: 26.2 us -> 22.9 us  [grads_call(): pl.pallas_call(functools.partial(grads_kernel, plan), in_specs=in_specs,...]
    unnamed x12 -> x8, local copies, waits for them, and re-layouts: 2.33 us -> 0.96 us
    all_to_all x1, waiting for transfers between devices: 0.8 us -> 1.65 us  [on_device(): lax.all_to_all(pairs, 'dp', split_axis=0, concat_axis=0, tiled=True, axis...]
    all_to_all x1, waiting for transfers between devices: 1.29 us -> 1.94 us  [on_device(): score_terms = exchange(scores)]
  transfers between devices with their start and end apart: 4 -> 4, of which waited for: 3 -> 4; matrix products, arithmetic and copies ran while one was open for 0% -> 0% of each run, Pallas kernels for 43% -> 39%
where the time goes in v2:
time: 59.2 us; the launch traced here: 58.4 us
  Pallas kernels  28.2 us (48%)
  starting transfers between devices  22.4 us (38%)
  waiting for transfers between devices  5.36 us (9%)
  local copies, waits for them, and re-layouts  1.68 us (3%)
  between operations  0.71 us (1%)
    pallas_call x3, Pallas kernels, grads_call(): pl.pallas_call(functools.partial(grads_kernel, plan), in_specs=in_specs,...  22.9 us
    all_to_all x1, starting transfers between devices, on_device(): lax.all_to_all(pairs, 'dp', split_axis=0, concat_axis=0, tiled=True, axis...  8.57 us
    all_to_all x1, starting transfers between devices, on_device(): parts = exchange(sent)  7.05 us
    all_to_all x1, starting transfers between devices, on_device(): score_terms = exchange(scores)  6.71 us
    pallas_call x1, Pallas kernels, act_parts(): pl.pallas_call(act_kernel, in_specs=[HBM] * 3, out_specs=VMEM, out_shape=...  3.02 us
    all_to_all x1, waiting for transfers between devices, on_device(): score_terms = exchange(scores)  1.94 us
    all_to_all x1, waiting for transfers between devices, on_device(): lax.all_to_all(pairs, 'dp', split_axis=0, concat_axis=0, tiled=True, axis...  1.65 us
    ppermute x1, waiting for transfers between devices, on_device(): other = lax.ppermute(terms, 'dp', [(i, i ^ 1) for i in range(16)])  1.24 us
  transfers between devices with their start and end apart: 4, of which 4 were waited for; matrix products, arithmetic and copies ran while one was open for 0% of the time, Pallas kernels for 39%

profile of v2, /device:TPU:32, one launch (start us, length us, event | category | flops | bytes accessed | tf_op | source)
XLA Modules:
  0.0 58.4 jit_solution(10646918557873296087)
XLA Ops:
  0.6 3.0 %act_parts.1 = f32[16,32,128]{2,1,0:T(8,128)} custom-call(bf16[688,1024]{1,0:T(8,128)(2,1)} %bitcast.8, bf16[688,1024]{1,0:T(8,128)(2,1)} %bitcast.12, bf16[64,688]{1,0:T(8,128)(2,1)} %bitcast.19), custom_call_target="tpu_custom_call" | custom-call | flops 90177536 | bytes 2818048 | tf_op jit(solution)/shard_map/act_parts/pallas_call | solution.py:101
  3.7 7.1 %all-to-all-start = ((f32[16,32,128]{2,1,0:T(8,128)}), f32[16,32,128]{2,1,0:T(8,128)S(1)}, u32[]{:S(2)}, u32[]{:S(2)}) async-start(f32[16,32,128]{2,1,0:T(8,128)} %act_parts.1), calls=%async_computation | async-start | bytes 524288 | tf_op jit(solution)/shard_map/all_to_all | solution.py:359
  10.7 0.0 copy-start.2
  10.7 8.2 %grads_0_0.1 = (bf16[688,1024]{1,0:T(8,128)(2,1)}, bf16[688,1024]{1,0:T(8,128)(2,1)}, f32[8,128]{1,0:T(8,128)}, bf16[128,1024]{1,0:T(8,128)(2,1)}) custom-call(bf16[1024,4096]{1,0:T(8,128)(2,1)} %grad_ref.5, bf16[688,4096]{1,0:T(8,128)(2,1)} %weight_ref.5, bf16[688,1024]{1,0:T(8,128)(2,1)} %bitcast.9, bf16[688,1024]{1,0:T(8,128)(2,1)} %bitcast.13, ...), custom_call_target="tpu_custom_call" | custom-call | flops 1610612736 | bytes 11534336 | tf_op jit(solution)/shard_map/grads_0_0/pallas_call | solution.py:252
  18.9 0.5 all-to-all-done.parts_ref
  19.4 0.0 copy-done.2
  19.4 0.0 copy-start
  19.4 0.9 %copy-done = bf16[128,1024]{1,0:T(8,128)(2,1)S(1)} copy-done((bf16[128,1024]{1,0:T(8,128)(2,1)S(1)}, bf16[128,1024]{1,0:T(8,128)(2,1)}, u32[]{:S(2)}) %copy-start) | copy-done | bytes 262168
  20.4 0.8 %example_terms.1 = f32[64,256]{1,0:T(8,128)S(1)} custom-call(f32[16,32,128]{2,1,0:T(8,128)S(1)} %all-to-all-done.parts_ref, s32[8,128]{1,0:T(8,128)S(1)} %bitcast.7, bf16[128,1024]{1,0:T(8,128)(2,1)S(1)} %copy-done), custom_call_target="tpu_custom_call" | custom-call | flops 100000000 | bytes 700000 | tf_op jit(solution)/shard_map/example_terms/pallas_call | solution.py:298
  21.2 0.1 collective-permute-start
  21.3 1.2 %collective-permute-done = f32[64,256]{1,0:T(8,128)S(1)} collective-permute-done((f32[64,256]{1,0:T(8,128)S(1)}, f32[64,256]{1,0:T(8,128)S(1)}, u32[]{:S(2)}, u32[]{:S(2)}) %collective-permute-start) | collective-permute-done | bytes 65568 | tf_op jit(solution)/shard_map/ppermute | solution.py:364
  22.5 0.0 copy-start.3
  22.5 0.7 %broadcast_in_dim.2 = bf16[8,64,256]{2,1,0:T(8,128)(2,1)} broadcast(bf16[64,256]{1,0:T(8,128)(2,1)S(1)} %add_convert_fusion.rest_2_), dimensions={1,2} | broadcast | bytes 294912 | tf_op jit(solution)/shard_map/broadcast_in_dim | solution.py:366
  23.2 8.6 %all-to-all-start.1 = ((bf16[8,64,256]{2,1,0:T(8,128)(2,1)}), bf16[8,64,256]{2,1,0:T(8,128)(2,1)S(1)}, u32[]{:S(2)}, u32[]{:S(2)}) async-start(bf16[8,64,256]{2,1,0:T(8,128)(2,1)} %broadcast_in_dim.2), calls=%async_computation.1 | async-start | bytes 524288 | tf_op jit(solution)/shard_map/all_to_all | solution.py:368
  31.8 0.0 copy-done.3
  31.8 0.0 copy-start.1
  31.8 9.1 %grads_192_0.1 = (bf16[688,1024]{1,0:T(8,128)(2,1)}, bf16[688,1024]{1,0:T(8,128)(2,1)}, f32[8,128]{1,0:T(8,128)}) custom-call(bf16[1024,4096]{1,0:T(8,128)(2,1)} %grad_ref.5, bf16[688,4096]{1,0:T(8,128)(2,1)} %weight_ref.5, bf16[688,1024]{1,0:T(8,128)(2,1)} %bitcast.10, bf16[688,1024]{1,0:T(8,128)(2,1)} %bitcast.14, ...), custom_call_target="tpu_custom_call", output_to_operand_aliasing={{0}: (4, {}), {1}: (5, {})} | custom-call | flops 3120562176 | bytes 13402112 | tf_op jit(solution)/shard_map/grads_192_0/pallas_call | solution.py:252
  40.9 1.7 %all-to-all-done.1.terms_ref = bf16[8,64,256]{2,1,0:T(8,128)(2,1)S(1)} async-done(((bf16[8,64,256]{2,1,0:T(8,128)(2,1)}), bf16[8,64,256]{2,1,0:T(8,128)(2,1)S(1)}, u32[]{:S(2)}, u32[]{:S(2)}) %all-to-all-start.1) | async-done | bytes 262176 | tf_op jit(solution)/shard_map/all_to_all | solution.py:368
  42.6 0.0 copy-done.1
  42.6 0.8 %score_parts.1.rest_2_ = f32[16,8,128]{2,1,0:T(8,128)} custom-call(bf16[8,64,256]{2,1,0:T(8,128)(2,1)S(1)} %all-to-all-done.1.terms_ref, bf16[256,256]{1,0:T(8,128)(2,1)S(1)} %copy-done.1), custom_call_target="tpu_custom_call" | custom-call | flops 10000000 | bytes 500000 | tf_op jit(solution)/shard_map/score_parts/pallas_call | solution.py:322
  43.4 6.7 %all-to-all-start.2 = ((f32[16,8,128]{2,1,0:T(8,128)}), f32[16,8,128]{2,1,0:T(8,128)S(1)}, u32[]{:S(2)}, u32[]{:S(2)}) async-start(f32[16,8,128]{2,1,0:T(8,128)} %score_parts.1.rest_2_), calls=%async_computation.2 | async-start | bytes 131072 | tf_op jit(solution)/shard_map/all_to_all | solution.py:375
  50.1 5.7 %grads_192_3.1 = (bf16[688,1024]{1,0:T(8,128)(2,1)}, bf16[688,1024]{1,0:T(8,128)(2,1)}, f32[8,128]{1,0:T(8,128)}) custom-call(bf16[1024,4096]{1,0:T(8,128)(2,1)} %grad_ref.5, bf16[688,4096]{1,0:T(8,128)(2,1)} %weight_ref.5, bf16[688,1024]{1,0:T(8,128)(2,1)} %bitcast.11, bf16[688,1024]{1,0:T(8,128)(2,1)} %bitcast.15, ...), custom_call_target="tpu_custom_call", output_to_operand_aliasing={{0}: (4, {}), {1}: (5, {})} | custom-call | flops 1040187392 | bytes 7176192 | tf_op jit(solution)/shard_map/grads_192_3/pallas_call | solution.py:252
  55.8 1.9 %all-to-all-done.2.parts_ref = f32[16,8,128]{2,1,0:T(8,128)S(1)} async-done(((f32[16,8,128]{2,1,0:T(8,128)}), f32[16,8,128]{2,1,0:T(8,128)S(1)}, u32[]{:S(2)}, u32[]{:S(2)}) %all-to-all-start.2) | async-done | bytes 65568 | tf_op jit(solution)/shard_map/all_to_all | solution.py:375
  57.8 0.6 %final_sum.1 = f32[4,256]{1,0:T(4,128)} custom-call(f32[16,8,128]{2,1,0:T(8,128)S(1)} %all-to-all-done.2.parts_ref), custom_call_target="tpu_custom_call" | custom-call | flops 100000 | bytes 70000 | tf_op jit(solution)/shard_map/final_sum/pallas_call | solution.py:342
  (1 shorter events, 0.0 us)
Async XLA Ops:
  3.7 15.8 %all-to-all-start = ((f32[16,32,128]{2,1,0:T(8,128)}), f32[16,32,128]{2,1,0:T(8,128)S(1)}, u32[]{:S(2)}, u32[]{:S(2)}) async-start(f32[16,32,128]{2,1,0:T(8,128)} %act_parts.1), calls=%async_computation | async-start | bytes 524288 | tf_op jit(solution)/shard_map/all_to_all | solution.py:359
  10.7 8.7 %copy-start.2 = (s32[1024]{0:T(1024)S(1)}, s32[1024]{0:T(1024)}, u32[]{:S(2)}) copy-start(s32[1024]{0:T(1024)} %param.14) | copy-start | bytes 12292
  19.4 1.0 %copy-start = (bf16[128,1024]{1,0:T(8,128)(2,1)S(1)}, bf16[128,1024]{1,0:T(8,128)(2,1)}, u32[]{:S(2)}) copy-start(bf16[128,1024]{1,0:T(8,128)(2,1)} %get-tuple-element.12.proj_ref) | copy-start | bytes 786436
  21.2 1.3 %collective-permute-start = (f32[64,256]{1,0:T(8,128)S(1)}, f32[64,256]{1,0:T(8,128)S(1)}, u32[]{:S(2)}, u32[]{:S(2)}) collective-permute-start(f32[64,256]{1,0:T(8,128)S(1)} %example_terms.1), channel_id=1, source_target_pairs={{0,16},{16,0},{32,48},{48,32},{64,80},{80,64},{96,112},{112,96},{1... | collective-permute-start | bytes 196616 | tf_op jit(solution)/shard_map/ppermute | solution.py:364
  22.5 9.3 %copy-start.3 = (bf16[64,256]{1,0:T(8,128)(2,1)}, bf16[64,256]{1,0:T(8,128)(2,1)S(1)}, u32[]{:S(2)}) copy-start(bf16[64,256]{1,0:T(8,128)(2,1)S(1)} %add_convert_fusion.rest_2_) | copy-start | bytes 98308
  23.2 19.3 %all-to-all-start.1 = ((bf16[8,64,256]{2,1,0:T(8,128)(2,1)}), bf16[8,64,256]{2,1,0:T(8,128)(2,1)S(1)}, u32[]{:S(2)}, u32[]{:S(2)}) async-start(bf16[8,64,256]{2,1,0:T(8,128)(2,1)} %broadcast_in_dim.2), calls=%async_computation.1 | async-start | bytes 524288 | tf_op jit(solution)/shard_map/all_to_all | solution.py:368
  31.8 10.7 %copy-start.1 = (bf16[256,256]{1,0:T(8,128)(2,1)S(1)}, bf16[256,256]{1,0:T(8,128)(2,1)}, u32[]{:S(2)}) copy-start(bf16[256,256]{1,0:T(8,128)(2,1)} %queries_ref.1) | copy-start | bytes 393220
  43.4 14.4 %all-to-all-start.2 = ((f32[16,8,128]{2,1,0:T(8,128)}), f32[16,8,128]{2,1,0:T(8,128)S(1)}, u32[]{:S(2)}, u32[]{:S(2)}) async-start(f32[16,8,128]{2,1,0:T(8,128)} %score_parts.1.rest_2_), calls=%async_computation.2 | async-start | bytes 131072 | tf_op jit(solution)/shard_map/all_to_all | solution.py:375

commit v3 on v2

v3 whole, which is shorter than its diff:
```python
import functools
import jax
import jax.numpy as jnp
from jax import lax
from jax.experimental import pallas as pl
from jax.experimental.pallas import tpu as pltpu
from jax.sharding import PartitionSpec as P

F32 = jnp.float32
BF16 = jnp.bfloat16
EXAMPLES = 64
MAX_COPIES = 80
ACT_PARTS = ((0, 256), (256, 256), (512, 176))
LIMIT = 60 << 20
OWN_TOKENS = 64
ROW_PARTS = ((0, 256), (256, 224), (480, 208))
LOADS = (
    ("grad", 0), ("weight", 0), ("grad", 1), ("weight", 1), ("value", 0), ("grad", 2), ("grad", 3),
    ("value", 1), ("weight", 2), ("value", 2),
)
BLOCKS = (
    ((("grad", 0), ("weight", 0)), ((0, 0),), ()),
    ((("grad", 1), ("weight", 1), ("value", 0)), ((0, 1), (1, 0), (1, 1)), ()),
    (
        (("grad", 2), ("grad", 3), ("value", 1)),
        ((0, 2), (1, 2), (0, 3), (1, 3)),
        (0, 1),
    ),
    ((("weight", 2), ("value", 2)), ((2, 0), (2, 1), (2, 2), (2, 3)), (2,)),
)
TOK_BLOCK = 256
NT = (((1,), (1,)), ((), ()))
HBM = pl.BlockSpec(memory_space=pltpu.HBM)
ANY = pl.BlockSpec(memory_space=pl.ANY)
VMEM = pl.BlockSpec(memory_space=pltpu.VMEM)
MIB = 1 << 20


def first_kernel(
    gate_ref, up_ref, act_proj_ref, grad_ref, grad_proj_ref, out_ref,
    gates, ups, act_projs, grads, grad_projs, sems,
):
    own = pl.multiple_of(lax.axis_index("tensor") * OWN_TOKENS, OWN_TOKENS)
    copies = [
        pltpu.make_async_copy(source, target, sems.at[index])
        for index, (source, target) in enumerate((
            (grad_proj_ref, grad_projs),
            (grad_ref.at[pl.ds(own, OWN_TOKENS), :], grads),
            (act_proj_ref, act_projs),
        ))
    ]
    value_copies = []
    for index, (start, rows) in enumerate(ACT_PARTS):
        part = pl.ds(start, rows)
        value_copies.append((
            pltpu.make_async_copy(gate_ref.at[part], gates.at[part], sems.at[3 + 2 * index]),
            pltpu.make_async_copy(up_ref.at[part], ups.at[part], sems.at[4 + 2 * index]),
        ))
    order = [part for pair in value_copies for part in pair]
    for part in order[:2] + copies + order[2:]:
        part.start()
    act = None
    for index, ((gate_copy, up_copy), (start, rows)) in enumerate(zip(value_copies, ACT_PARTS)):
        gate_copy.wait()
        up_copy.wait()
        if index == 0:
            for part in copies:
                part.wait()
            projected = lax.dot_general(
                grads[...], grad_projs[...], NT, preferred_element_type=F32
            )
            half = OWN_TOKENS // 2
            packed = jnp.concatenate([projected[:half], projected[half:]], axis=1).astype(BF16)
            for part in range(16):
                out_ref[part, 32:, :] = packed
        gate = gates[start:start + rows, :].astype(F32)
        up = ups[start:start + rows, :].astype(F32)
        hidden = (gate * jax.nn.sigmoid(gate) * up).astype(BF16)
        term = jnp.dot(act_projs[:, start:start + rows], hidden, preferred_element_type=F32)
        act = term if act is None else act + term
    for part in range(16):
        blocks = [
            act[4 * part:4 * part + 4, 128 * block:128 * block + 128] for block in range(8)
        ]
        out_ref[part, :32, :] = jnp.concatenate(blocks, axis=0).astype(BF16)


def first_parts(gate, up, act_proj, grad, grad_proj):
    hidden_units, tokens = gate.shape
    ranks, width = grad_proj.shape
    return pl.pallas_call(
        first_kernel,
        in_specs=[HBM] * 5,
        out_specs=VMEM,
        out_shape=jax.ShapeDtypeStruct((16, 64, 128), BF16),
        scratch_shapes=[
            pltpu.VMEM(gate.shape, BF16),
            pltpu.VMEM(gate.shape, BF16),
            pltpu.VMEM(act_proj.shape, BF16),
            pltpu.VMEM((OWN_TOKENS, width), BF16),
            pltpu.VMEM(grad_proj.shape, BF16),
            pltpu.SemaphoreType.DMA((3 + 2 * len(ACT_PARTS),)),
        ],
        compiler_params=pltpu.CompilerParams(vmem_limit_bytes=LIMIT),
        cost_estimate=pl.CostEstimate(
            flops=2 * ranks * hidden_units * tokens,
            bytes_accessed=4 * hidden_units * tokens,
            transcendentals=hidden_units * tokens,
        ),
        name="first_parts",
    )(gate, up, act_proj, grad, grad_proj)


def grads_kernel(
    grad_ref, weight_ref, gate_ref, up_ref, _after, gate_out, up_out,
    grads, weights, gates, ups, gate_done, up_done, products, sems,
):
    sem = iter(range(MAX_COPIES))
    copies = {}

    def start(key, *pairs):
        for source, target in pairs:
            part = pltpu.make_async_copy(source, target, sems.at[next(sem)])
            part.start()
            copies.setdefault(key, []).append(part)

    def wait(*keys):
        for key in keys:
            for part in copies.pop(key):
                part.wait()

    def load(kind, part):
        if kind == "grad":
            rows = pl.ds(TOK_BLOCK * part, TOK_BLOCK)
            start((kind, part), (grad_ref.at[rows, :], grads.at[rows, :]))
            return
        rows = pl.ds(*ROW_PARTS[part])
        if kind == "weight":
            start((kind, part), (weight_ref.at[rows, :], weights.at[rows, :]))
        else:
            start(
                (kind, part),
                (gate_ref.at[rows, :], gates.at[rows, :]),
                (up_ref.at[rows, :], ups.at[rows, :]),
            )

    def multiply(row_part, tok_part):
        rows, tok = pl.ds(*ROW_PARTS[row_part]), pl.ds(TOK_BLOCK * tok_part, TOK_BLOCK)
        products[rows, tok] = lax.dot_general(
            weights[rows, :], grads[tok, :], NT, preferred_element_type=F32
        )

    def finish(row_part, tok_part):
        here = (pl.ds(*ROW_PARTS[row_part]), pl.ds(TOK_BLOCK * tok_part, TOK_BLOCK))
        gate = gates[here].astype(F32)
        sig = jax.nn.sigmoid(gate)
        scaled = products[here] * sig
        up_done[here] = (scaled * gate).astype(BF16)
        gate_done[here] = (
            scaled * ups[here].astype(F32) * (1.0 + gate * (1.0 - sig))
        ).astype(BF16)

    def store(row_part):
        rows = pl.ds(*ROW_PARTS[row_part])
        start(
            "out",
            (gate_done.at[rows, :], gate_out.at[rows, :]),
            (up_done.at[rows, :], up_out.at[rows, :]),
        )

    for kind, part in LOADS:
        load(kind, part)
    pending = []
    for needs, tiles, rows_done in BLOCKS:
        wait(*needs)
        for tile in tiles:
            multiply(*tile)
            pending.append(tile)
            while len(pending) > 1 and ("value", pending[0][0]) not in copies:
                finish(*pending.pop(0))
        if rows_done:
            while pending:
                finish(*pending.pop(0))
        for row_part in rows_done:
            store(row_part)
    wait("out")


def grads_call(grad, weight, gate, up, after):
    tokens, width = grad.shape
    rows = gate.shape[0]
    return pl.pallas_call(
        grads_kernel,
        in_specs=[HBM] * 4 + [ANY],
        out_specs=[HBM] * 2,
        out_shape=[jax.ShapeDtypeStruct(gate.shape, BF16)] * 2,
        scratch_shapes=[
            pltpu.VMEM((tokens, width), BF16),
            pltpu.VMEM((rows, width), BF16),
            *[pltpu.VMEM((rows, tokens), BF16)] * 4,
            pltpu.VMEM((rows, tokens), F32),
            pltpu.SemaphoreType.DMA((MAX_COPIES,)),
        ],
        compiler_params=pltpu.CompilerParams(vmem_limit_bytes=LIMIT),
        cost_estimate=pl.CostEstimate(
            flops=2 * rows * tokens * width,
            bytes_accessed=2 * (tokens + rows) * width + 8 * rows * tokens,
            transcendentals=rows * tokens,
        ),
        name="grads",
    )(grad, weight, gate, up, after)


def example_kernel(parts_ref, ids_ref, out_ref):
    act = parts_ref[0, :32, :].astype(F32)
    for part in range(1, 16):
        act = act + parts_ref[part, :32, :].astype(F32)
    projected = []
    for part in range(16):
        packed = parts_ref[part, 32:, :]
        projected += [packed[:, :64], packed[:, 64:]]
    projected = jnp.concatenate(projected, axis=0)
    example = lax.broadcasted_iota(jnp.int32, (EXAMPLES, 128), 0)
    members = [ids_ref[block:block + 1, :] == example for block in range(8)]
    weighted = jnp.concatenate(
        [
            jnp.concatenate(
                [
                    jnp.where(members[block], act[4 * block + rank:4 * block + rank + 1, :], 0.0)
                    for block in range(8)
                ],
                axis=1,
            )
            for rank in range(4)
        ],
        axis=0,
    )
    high = weighted.astype(BF16)
    low = (weighted - high.astype(F32)).astype(BF16)
    terms = jnp.dot(high, projected, preferred_element_type=F32) + jnp.dot(
        low, projected, preferred_element_type=F32
    )
    for rank in range(4):
        out_ref[:, 64 * rank:64 * rank + 64] = terms[EXAMPLES * rank:EXAMPLES * (rank + 1)]


def example_terms(parts, ids):
    return pl.pallas_call(
        example_kernel,
        out_shape=jax.ShapeDtypeStruct((EXAMPLES, 256), F32),
        compiler_params=pltpu.CompilerParams(vmem_limit_bytes=16 * MIB),
        cost_estimate=pl.CostEstimate(flops=100_000_000, bytes_accessed=700_000, transcendentals=0),
        name="example_terms",
    )(parts, ids)


def score_kernel(terms_ref, queries_ref, out_ref):
    total = terms_ref[0].astype(F32)
    for part in range(1, 8):
        total = total + terms_ref[part].astype(F32)
    scores = lax.dot_general(
        total.astype(BF16), queries_ref[...], NT, preferred_element_type=F32
    )
    for part in range(16):
        for half in range(2):
            out_ref[part, 4 * half:4 * half + 4, :] = scores[
                4 * part:4 * part + 4, 128 * half:128 * half + 128
            ]


def score_parts(terms, queries):
    return pl.pallas_call(
        score_kernel,
        in_specs=[VMEM, VMEM],
        out_specs=VMEM,
        out_shape=jax.ShapeDtypeStruct((16, 8, 128), F32),
        compiler_params=pltpu.CompilerParams(vmem_limit_bytes=16 * MIB),
        cost_estimate=pl.CostEstimate(flops=10_000_000, bytes_accessed=500_000, transcendentals=0),
        name="score_parts",
    )(terms, queries)


def final_kernel(parts_ref, out_ref):
    total = parts_ref[0]
    for part in range(1, 16):
        total = total + parts_ref[part]
    out_ref[:, :128] = total[:4]
    out_ref[:, 128:] = total[4:]


def final_sum(parts):
    return pl.pallas_call(
        final_kernel,
        in_specs=[VMEM],
        out_specs=VMEM,
        out_shape=jax.ShapeDtypeStruct((4, 256), F32),
        compiler_params=pltpu.CompilerParams(vmem_limit_bytes=16 * MIB),
        cost_estimate=pl.CostEstimate(flops=100_000, bytes_accessed=70_000, transcendentals=0),
        name="final_sum",
    )(parts)


def on_device(out_grad, gate_pre, up_pre, down_weight, proj_hidden, proj_out, example_ids, queries):
    gate, up = gate_pre.T, up_pre.T
    exchange = functools.partial(
        lax.all_to_all, axis_name="tensor", split_axis=0, concat_axis=0, tiled=True
    )
    parts = exchange(first_parts(gate, up, proj_hidden.T, out_grad, proj_out.T))
    terms = example_terms(parts, example_ids.reshape(8, 128))
    other = lax.ppermute(terms, "dp", [(i, i ^ 1) for i in range(16)])
    pair = (terms + other).astype(BF16)
    pairs = jnp.broadcast_to(pair[None], (8, *pair.shape))
    chips = [[2 * z + core for z in range(8)] for core in range(2)]
    all_terms = lax.all_to_all(
        pairs, "dp", split_axis=0, concat_axis=0, tiled=True, axis_index_groups=chips
    )
    gate_grad, up_grad = grads_call(out_grad, down_weight, gate, up, pair)
    all_terms, gate_grad = lax.optimization_barrier((all_terms, gate_grad))
    score_terms = exchange(score_parts(all_terms, queries))
    return gate_grad.T, up_grad.T, final_sum(score_terms)


def solution(mesh):
    in_specs = (
        P("dp", None),
        P("dp", "tensor"),
        P("dp", "tensor"),
        P("tensor", None),
        P("tensor", None),
        P(),
        P("dp"),
        P("dp", "tensor"),
    )
    out_specs = (P("dp", "tensor"), P("dp", "tensor"), P("tensor", "dp"))
    return jax.shard_map(
        on_device, mesh=mesh, in_specs=in_specs, out_specs=out_specs, check_vma=False
    )
```

time: 59.2 us -> 56.7 us (0.958)
  blocking collectives: 0 us -> 26.3 us
  starting transfers between devices: 22.4 us -> 8.65 us
  Pallas kernels: 28.2 us -> 18.8 us
  waiting for transfers between devices: 5.36 us -> 1.24 us
  local copies, waits for them, and re-layouts: 1.68 us -> 0.73 us
    all_to_all x0 -> x2, blocking collectives: none -> 26.3 us  [the longest x1 15.7 us: on_device(): parts = exchange(first_parts(gate, up, proj_hidden.T, out_grad, proj_out.T))]
    all_to_all x2 -> x0, starting transfers between devices: 13.8 us -> none  [the longest x1 7.05 us: on_device(): parts = exchange(sent)]
    pallas_call x4 -> x2, Pallas kernels: 26 us -> 17.4 us  [the longest x1 13.6 us: grads_call(): pl.pallas_call(grads_kernel, in_specs=[HBM] * 4 + [ANY], out_specs=[HBM]...]
    all_to_all x2 -> x0, waiting for transfers between devices: 2.47 us -> none  [the longest x1 1.94 us: on_device(): score_terms = exchange(scores)]
    all_to_all x1, waiting for transfers between devices: 1.65 us -> 0.01 us  [on_device(): lax.all_to_all(pairs, 'dp', split_axis=0, concat_axis=0, tiled=True, axis...]
    unnamed x8 -> x6, local copies, waits for them, and re-layouts: 0.96 us -> 0.01 us
    pallas_call x1, Pallas kernels: 0.81 us -> 0.18 us  [score_parts(): pl.pallas_call(score_kernel, in_specs=[VMEM, VMEM], out_specs=VMEM, out_s...]
  transfers between devices with their start and end apart: 4 -> 2, of which waited for: 4 -> 1; matrix products, arithmetic and copies ran while one was open for 0% -> 0% of each run, Pallas kernels for 39% -> 24%
where the time goes in v3:
time: 56.7 us; the launch traced here: 56.4 us
  blocking collectives  26.3 us (46%)
  Pallas kernels  18.8 us (33%)
  starting transfers between devices  8.65 us (15%)
  waiting for transfers between devices  1.24 us (2%)
  local copies, waits for them, and re-layouts  0.73 us (1%)
  between operations  0.69 us (1%)
    all_to_all x1, blocking collectives, on_device(): parts = exchange(first_parts(gate, up, proj_hidden.T, out_grad, proj_out.T))  15.7 us
    pallas_call x1, Pallas kernels, grads_call(): pl.pallas_call(grads_kernel, in_specs=[HBM] * 4 + [ANY], out_specs=[HBM]...  13.6 us
    all_to_all x1, blocking collectives, on_device(): score_terms = exchange(score_parts(all_terms, queries))  10.6 us
    all_to_all x1, starting transfers between devices, on_device(): lax.all_to_all(pairs, 'dp', split_axis=0, concat_axis=0, tiled=True, axis...  8.57 us
    pallas_call x1, Pallas kernels, first_parts(): pl.pallas_call(first_kernel, in_specs=[HBM] * 5, out_specs=VMEM, out_shap...  3.84 us
    ppermute x1, waiting for transfers between devices, on_device(): other = lax.ppermute(terms, 'dp', [(i, i ^ 1) for i in range(16)])  1.24 us
  transfers between devices with their start and end apart: 2, of which 1 were waited for; matrix products, arithmetic and copies ran while one was open for 0% of the time, Pallas kernels for 24%

profile of v3, /device:TPU:32, one launch (start us, length us, event | category | flops | bytes accessed | tf_op | source)
XLA Modules:
  0.0 56.4 jit_solution(8246196420919166984)
XLA Ops:
  0.6 0.0 copy-start.1
  0.6 3.8 %first_parts.1 = bf16[16,64,128]{2,1,0:T(8,128)(2,1)} custom-call(bf16[688,1024]{1,0:T(8,128)(2,1)} %bitcast.8, bf16[688,1024]{1,0:T(8,128)(2,1)} %bitcast.10, bf16[64,688]{1,0:T(8,128)(2,1)} %bitcast.13, bf16[1024,4096]{1,0:T(8,128)(2,1)} %grad_ref.3, bf16[64,4096]{1,0:T(8,128)(2,1)} %bitcast.12), custom_call_target="tpu_custom_call" | custom-call | flops 90177536 | bytes 2818048 | tf_op jit(solution)/shard_map/first_parts/pallas_call | solution.py:91
  4.5 15.7 %all_to_all.15.parts_ref = bf16[16,64,128]{2,1,0:T(8,128)(2,1)S(1)} all-to-all(bf16[16,64,128]{2,1,0:T(8,128)(2,1)} %first_parts.1), channel_id=1, replica_groups=mesh['dp'=16,'tensor'=16] {'tensor'}, dimensions={0} | all-to-all | bytes 524288 | tf_op jit(solution)/shard_map/all_to_all | solution.py:308
  20.2 0.0 copy-done.1
  20.2 0.6 %example_terms.1 = f32[64,256]{1,0:T(8,128)S(1)} custom-call(bf16[16,64,128]{2,1,0:T(8,128)(2,1)S(1)} %all_to_all.15.parts_ref, s32[8,128]{1,0:T(8,128)S(1)} %bitcast.7), custom_call_target="tpu_custom_call" | custom-call | flops 100000000 | bytes 700000 | tf_op jit(solution)/shard_map/example_terms/pallas_call | solution.py:248
  20.8 0.1 collective-permute-start
  20.9 1.2 %collective-permute-done = f32[64,256]{1,0:T(8,128)S(1)} collective-permute-done((f32[64,256]{1,0:T(8,128)S(1)}, f32[64,256]{1,0:T(8,128)S(1)}, u32[]{:S(2)}, u32[]{:S(2)}) %collective-permute-start) | collective-permute-done | bytes 65568 | tf_op jit(solution)/shard_map/ppermute | solution.py:310
  22.1 0.0 copy-start.2
  22.2 0.7 %broadcast_in_dim.2 = bf16[8,64,256]{2,1,0:T(8,128)(2,1)} broadcast(bf16[64,256]{1,0:T(8,128)(2,1)S(1)} %add_convert_fusion._after), dimensions={1,2} | broadcast | bytes 294912 | tf_op jit(solution)/shard_map/broadcast_in_dim | solution.py:312
  22.9 8.6 %all-to-all-start.1 = ((bf16[8,64,256]{2,1,0:T(8,128)(2,1)}), bf16[8,64,256]{2,1,0:T(8,128)(2,1)S(1)}, u32[]{:S(2)}, u32[]{:S(2)}) async-start(bf16[8,64,256]{2,1,0:T(8,128)(2,1)} %broadcast_in_dim.2), calls=%async_computation.1 | async-start | bytes 524288 | tf_op jit(solution)/shard_map/all_to_all | solution.py:314
  31.4 0.0 copy-done.2
  31.5 0.0 copy-start
  31.5 13.6 %grads.1 = (bf16[688,1024]{1,0:T(8,128)(2,1)}, bf16[688,1024]{1,0:T(8,128)(2,1)}) custom-call(bf16[1024,4096]{1,0:T(8,128)(2,1)} %grad_ref.3, bf16[688,4096]{1,0:T(8,128)(2,1)} %weight_ref.1, bf16[688,1024]{1,0:T(8,128)(2,1)} %bitcast.9, bf16[688,1024]{1,0:T(8,128)(2,1)} %bitcast.11, bf16[64,256]{1,0:T(8,128)(2,1)} %copy-done.2), custom_call_target="tpu_custom_call" | custom-call | flops 5771362304 | bytes 19660800 | tf_op jit(solution)/shard_map/grads/pallas_call | solution.py:192
  45.0 0.0 all-to-all-done.1.terms_ref
  45.0 0.0 copy-done
  45.1 0.2 score_parts.1
  45.2 10.6 %all_to_all.16.parts_ref = f32[16,8,128]{2,1,0:T(8,128)S(1)} all-to-all(f32[16,8,128]{2,1,0:T(8,128)S(1)} %score_parts.1), channel_id=1, replica_groups=mesh['dp'=16,'tensor'=16] {'tensor'}, dimensions={0} | all-to-all | bytes 131072 | tf_op jit(solution)/shard_map/all_to_all | solution.py:319
  55.8 0.6 %final_sum.1 = f32[4,256]{1,0:T(4,128)} custom-call(f32[16,8,128]{2,1,0:T(8,128)S(1)} %all_to_all.16.parts_ref), custom_call_target="tpu_custom_call" | custom-call | flops 100000 | bytes 70000 | tf_op jit(solution)/shard_map/final_sum/pallas_call | solution.py:292
  (1 shorter events, 0.0 us)
Async XLA Ops:
  0.6 19.6 %copy-start.1 = (s32[1024]{0:T(1024)S(1)}, s32[1024]{0:T(1024)}, u32[]{:S(2)}) copy-start(s32[1024]{0:T(1024)} %param.14) | copy-start | bytes 12292
  20.8 1.3 %collective-permute-start = (f32[64,256]{1,0:T(8,128)S(1)}, f32[64,256]{1,0:T(8,128)S(1)}, u32[]{:S(2)}, u32[]{:S(2)}) collective-permute-start(f32[64,256]{1,0:T(8,128)S(1)} %example_terms.1), channel_id=1, source_target_pairs={{0,16},{16,0},{32,48},{48,32},{64,80},{80,64},{96,112},{112,96},{1... | collective-permute-start | bytes 196616 | tf_op jit(solution)/shard_map/ppermute | solution.py:310
  22.1 9.3 %copy-start.2 = (bf16[64,256]{1,0:T(8,128)(2,1)}, bf16[64,256]{1,0:T(8,128)(2,1)S(1)}, u32[]{:S(2)}) copy-start(bf16[64,256]{1,0:T(8,128)(2,1)S(1)} %add_convert_fusion._after) | copy-start | bytes 98308
  22.9 22.2 %all-to-all-start.1 = ((bf16[8,64,256]{2,1,0:T(8,128)(2,1)}), bf16[8,64,256]{2,1,0:T(8,128)(2,1)S(1)}, u32[]{:S(2)}, u32[]{:S(2)}) async-start(bf16[8,64,256]{2,1,0:T(8,128)(2,1)} %broadcast_in_dim.2), calls=%async_computation.1 | async-start | bytes 524288 | tf_op jit(solution)/shard_map/all_to_all | solution.py:314
  31.5 13.6 %copy-start = (bf16[256,256]{1,0:T(8,128)(2,1)S(1)}, bf16[256,256]{1,0:T(8,128)(2,1)}, u32[]{:S(2)}) copy-start(bf16[256,256]{1,0:T(8,128)(2,1)} %queries_ref.1) | copy-start | bytes 393220

commit v4 on v3

--- a/solution.py
+++ b/solution.py
@@ -10,7 +10,7 @@
 BF16 = jnp.bfloat16
 EXAMPLES = 64
 MAX_COPIES = 80
-ACT_PARTS = ((0, 256), (256, 256), (512, 176))
+ACT_PARTS = ((0, 128), (128, 256), (384, 256), (640, 48))
 LIMIT = 60 << 20
 OWN_TOKENS = 64
 ROW_PARTS = ((0, 256), (256, 224), (480, 208))
@@ -57,7 +57,7 @@
             pltpu.make_async_copy(up_ref.at[part], ups.at[part], sems.at[4 + 2 * index]),
         ))
     order = [part for pair in value_copies for part in pair]
-    for part in order[:2] + copies + order[2:]:
+    for part in copies + order:
         part.start()
     act = None
     for index, ((gate_copy, up_copy), (start, rows)) in enumerate(zip(value_copies, ACT_PARTS)):

time: 56.7 us -> 56.4 us (level)
  no operation moved by 1% of the time
where the time goes in v4:
time: 56.4 us; the launch traced here: 56.1 us
  blocking collectives  26.3 us (47%)
  Pallas kernels  18.5 us (33%)
  starting transfers between devices  8.65 us (15%)
  waiting for transfers between devices  1.24 us (2%)
  local copies, waits for them, and re-layouts  0.73 us (1%)
  between operations  0.69 us (1%)
    all_to_all x1, blocking collectives, on_device(): parts = exchange(first_parts(gate, up, proj_hidden.T, out_grad, proj_out.T))  15.7 us
    pallas_call x1, Pallas kernels, grads_call(): pl.pallas_call(grads_kernel, in_specs=[HBM] * 4 + [ANY], out_specs=[HBM]...  13.6 us
    all_to_all x1, blocking collectives, on_device(): score_terms = exchange(score_parts(all_terms, queries))  10.6 us
    all_to_all x1, starting transfers between devices, on_device(): lax.all_to_all(pairs, 'dp', split_axis=0, concat_axis=0, tiled=True, axis...  8.57 us
    pallas_call x1, Pallas kernels, first_parts(): pl.pallas_call(first_kernel, in_specs=[HBM] * 5, out_specs=VMEM, out_shap...  3.54 us
    ppermute x1, waiting for transfers between devices, on_device(): other = lax.ppermute(terms, 'dp', [(i, i ^ 1) for i in range(16)])  1.24 us
  transfers between devices with their start and end apart: 2, of which 1 were waited for; matrix products, arithmetic and copies ran while one was open for 0% of the time, Pallas kernels for 24%

profile of v4, /device:TPU:32, one launch (start us, length us, event | category | flops | bytes accessed | tf_op | source)
XLA Modules:
  0.0 56.1 jit_solution(14673250899481925755)
XLA Ops:
  0.6 0.0 copy-start.1
  0.6 3.5 %first_parts.1 = bf16[16,64,128]{2,1,0:T(8,128)(2,1)} custom-call(bf16[688,1024]{1,0:T(8,128)(2,1)} %bitcast.8, bf16[688,1024]{1,0:T(8,128)(2,1)} %bitcast.10, bf16[64,688]{1,0:T(8,128)(2,1)} %bitcast.13, bf16[1024,4096]{1,0:T(8,128)(2,1)} %grad_ref.3, bf16[64,4096]{1,0:T(8,128)(2,1)} %bitcast.12), custom_call_target="tpu_custom_call" | custom-call | flops 90177536 | bytes 2818048 | tf_op jit(solution)/shard_map/first_parts/pallas_call | solution.py:91
  4.2 15.7 %all_to_all.15.parts_ref = bf16[16,64,128]{2,1,0:T(8,128)(2,1)S(1)} all-to-all(bf16[16,64,128]{2,1,0:T(8,128)(2,1)} %first_parts.1), channel_id=1, replica_groups=mesh['dp'=16,'tensor'=16] {'tensor'}, dimensions={0} | all-to-all | bytes 524288 | tf_op jit(solution)/shard_map/all_to_all | solution.py:308
  19.9 0.0 copy-done.1
  19.9 0.6 %example_terms.1 = f32[64,256]{1,0:T(8,128)S(1)} custom-call(bf16[16,64,128]{2,1,0:T(8,128)(2,1)S(1)} %all_to_all.15.parts_ref, s32[8,128]{1,0:T(8,128)S(1)} %bitcast.7), custom_call_target="tpu_custom_call" | custom-call | flops 100000000 | bytes 700000 | tf_op jit(solution)/shard_map/example_terms/pallas_call | solution.py:248
  20.5 0.1 collective-permute-start
  20.6 1.2 %collective-permute-done = f32[64,256]{1,0:T(8,128)S(1)} collective-permute-done((f32[64,256]{1,0:T(8,128)S(1)}, f32[64,256]{1,0:T(8,128)S(1)}, u32[]{:S(2)}, u32[]{:S(2)}) %collective-permute-start) | collective-permute-done | bytes 65568 | tf_op jit(solution)/shard_map/ppermute | solution.py:310
  21.8 0.0 copy-start.2
  21.9 0.7 %broadcast_in_dim.2 = bf16[8,64,256]{2,1,0:T(8,128)(2,1)} broadcast(bf16[64,256]{1,0:T(8,128)(2,1)S(1)} %add_convert_fusion._after), dimensions={1,2} | broadcast | bytes 294912 | tf_op jit(solution)/shard_map/broadcast_in_dim | solution.py:312
  22.6 8.6 %all-to-all-start.1 = ((bf16[8,64,256]{2,1,0:T(8,128)(2,1)}), bf16[8,64,256]{2,1,0:T(8,128)(2,1)S(1)}, u32[]{:S(2)}, u32[]{:S(2)}) async-start(bf16[8,64,256]{2,1,0:T(8,128)(2,1)} %broadcast_in_dim.2), calls=%async_computation.1 | async-start | bytes 524288 | tf_op jit(solution)/shard_map/all_to_all | solution.py:314
  31.1 0.0 copy-done.2
  31.1 0.0 copy-start
  31.1 13.6 %grads.1 = (bf16[688,1024]{1,0:T(8,128)(2,1)}, bf16[688,1024]{1,0:T(8,128)(2,1)}) custom-call(bf16[1024,4096]{1,0:T(8,128)(2,1)} %grad_ref.3, bf16[688,4096]{1,0:T(8,128)(2,1)} %weight_ref.1, bf16[688,1024]{1,0:T(8,128)(2,1)} %bitcast.9, bf16[688,1024]{1,0:T(8,128)(2,1)} %bitcast.11, bf16[64,256]{1,0:T(8,128)(2,1)} %copy-done.2), custom_call_target="tpu_custom_call" | custom-call | flops 5771362304 | bytes 19660800 | tf_op jit(solution)/shard_map/grads/pallas_call | solution.py:192
  44.7 0.0 all-to-all-done.1.terms_ref
  44.7 0.0 copy-done
  44.7 0.2 score_parts.1
  44.9 10.6 %all_to_all.16.parts_ref = f32[16,8,128]{2,1,0:T(8,128)S(1)} all-to-all(f32[16,8,128]{2,1,0:T(8,128)S(1)} %score_parts.1), channel_id=1, replica_groups=mesh['dp'=16,'tensor'=16] {'tensor'}, dimensions={0} | all-to-all | bytes 131072 | tf_op jit(solution)/shard_map/all_to_all | solution.py:319
  55.5 0.6 %final_sum.1 = f32[4,256]{1,0:T(4,128)} custom-call(f32[16,8,128]{2,1,0:T(8,128)S(1)} %all_to_all.16.parts_ref), custom_call_target="tpu_custom_call" | custom-call | flops 100000 | bytes 70000 | tf_op jit(solution)/shard_map/final_sum/pallas_call | solution.py:292
  (1 shorter events, 0.0 us)
Async XLA Ops:
  0.6 19.3 %copy-start.1 = (s32[1024]{0:T(1024)S(1)}, s32[1024]{0:T(1024)}, u32[]{:S(2)}) copy-start(s32[1024]{0:T(1024)} %param.14) | copy-start | bytes 12292
  20.5 1.3 %collective-permute-start = (f32[64,256]{1,0:T(8,128)S(1)}, f32[64,256]{1,0:T(8,128)S(1)}, u32[]{:S(2)}, u32[]{:S(2)}) collective-permute-start(f32[64,256]{1,0:T(8,128)S(1)} %example_terms.1), channel_id=1, source_target_pairs={{0,16},{16,0},{32,48},{48,32},{64,80},{80,64},{96,112},{112,96},{1... | collective-permute-start | bytes 196616 | tf_op jit(solution)/shard_map/ppermute | solution.py:310
  21.8 9.3 %copy-start.2 = (bf16[64,256]{1,0:T(8,128)(2,1)}, bf16[64,256]{1,0:T(8,128)(2,1)S(1)}, u32[]{:S(2)}) copy-start(bf16[64,256]{1,0:T(8,128)(2,1)S(1)} %add_convert_fusion._after) | copy-start | bytes 98308
  22.6 22.1 %all-to-all-start.1 = ((bf16[8,64,256]{2,1,0:T(8,128)(2,1)}), bf16[8,64,256]{2,1,0:T(8,128)(2,1)S(1)}, u32[]{:S(2)}, u32[]{:S(2)}) async-start(bf16[8,64,256]{2,1,0:T(8,128)(2,1)} %broadcast_in_dim.2), calls=%async_computation.1 | async-start | bytes 524288 | tf_op jit(solution)/shard_map/all_to_all | solution.py:314
  31.1 13.6 %copy-start = (bf16[256,256]{1,0:T(8,128)(2,1)S(1)}, bf16[256,256]{1,0:T(8,128)(2,1)}, u32[]{:S(2)}) copy-start(bf16[256,256]{1,0:T(8,128)(2,1)} %queries_ref.1) | copy-start | bytes 393220

commit v5 on v4

--- a/solution.py
+++ b/solution.py
@@ -146,9 +146,12 @@
 
     def multiply(row_part, tok_part):
         rows, tok = pl.ds(*ROW_PARTS[row_part]), pl.ds(TOK_BLOCK * tok_part, TOK_BLOCK)
-        products[rows, tok] = lax.dot_general(
-            weights[rows, :], grads[tok, :], NT, preferred_element_type=F32
+        row, size = ROW_PARTS[row_part]
+        lead = 256 - size
+        product = lax.dot_general(
+            weights[pl.ds(row - lead, 256), :], grads[tok, :], NT, preferred_element_type=F32
         )
+        products[rows, tok] = product[lead:]
 
     def finish(row_part, tok_part):
         here = (pl.ds(*ROW_PARTS[row_part]), pl.ds(TOK_BLOCK * tok_part, TOK_BLOCK))

time: 56.4 us -> 56.1 us (level)
  no operation moved by 1% of the time
where the time goes in v5:
time: 56.1 us; the launch traced here: 55.8 us
  blocking collectives  26.3 us (47%)
  Pallas kernels  18.1 us (32%)
  starting transfers between devices  8.65 us (15%)
  waiting for transfers between devices  1.24 us (2%)
  local copies, waits for them, and re-layouts  0.73 us (1%)
  between operations  0.69 us (1%)
    all_to_all x1, blocking collectives, on_device(): parts = exchange(first_parts(gate, up, proj_hidden.T, out_grad, proj_out.T))  15.7 us
    pallas_call x1, Pallas kernels, grads_call(): pl.pallas_call(grads_kernel, in_specs=[HBM] * 4 + [ANY], out_specs=[HBM]...  13.2 us
    all_to_all x1, blocking collectives, on_device(): score_terms = exchange(score_parts(all_terms, queries))  10.6 us
    all_to_all x1, starting transfers between devices, on_device(): lax.all_to_all(pairs, 'dp', split_axis=0, concat_axis=0, tiled=True, axis...  8.57 us
    pallas_call x1, Pallas kernels, first_parts(): pl.pallas_call(first_kernel, in_specs=[HBM] * 5, out_specs=VMEM, out_shap...  3.54 us
    ppermute x1, waiting for transfers between devices, on_device(): other = lax.ppermute(terms, 'dp', [(i, i ^ 1) for i in range(16)])  1.24 us
  transfers between devices with their start and end apart: 2, of which 1 were waited for; matrix products, arithmetic and copies ran while one was open for 0% of the time, Pallas kernels for 24%

profile of v5, /device:TPU:32, one launch (start us, length us, event | category | flops | bytes accessed | tf_op | source)
XLA Modules:
  0.0 55.8 jit_solution(6001864439518279254)
XLA Ops:
  0.6 0.0 copy-start.1
  0.6 3.5 %first_parts.1 = bf16[16,64,128]{2,1,0:T(8,128)(2,1)} custom-call(bf16[688,1024]{1,0:T(8,128)(2,1)} %bitcast.8, bf16[688,1024]{1,0:T(8,128)(2,1)} %bitcast.10, bf16[64,688]{1,0:T(8,128)(2,1)} %bitcast.13, bf16[1024,4096]{1,0:T(8,128)(2,1)} %grad_ref.3, bf16[64,4096]{1,0:T(8,128)(2,1)} %bitcast.12), custom_call_target="tpu_custom_call" | custom-call | flops 90177536 | bytes 2818048 | tf_op jit(solution)/shard_map/first_parts/pallas_call | solution.py:91
  4.2 15.7 %all_to_all.15.parts_ref = bf16[16,64,128]{2,1,0:T(8,128)(2,1)S(1)} all-to-all(bf16[16,64,128]{2,1,0:T(8,128)(2,1)} %first_parts.1), channel_id=1, replica_groups=mesh['dp'=16,'tensor'=16] {'tensor'}, dimensions={0} | all-to-all | bytes 524288 | tf_op jit(solution)/shard_map/all_to_all | solution.py:311
  19.9 0.0 copy-done.1
  19.9 0.6 %example_terms.1 = f32[64,256]{1,0:T(8,128)S(1)} custom-call(bf16[16,64,128]{2,1,0:T(8,128)(2,1)S(1)} %all_to_all.15.parts_ref, s32[8,128]{1,0:T(8,128)S(1)} %bitcast.7), custom_call_target="tpu_custom_call" | custom-call | flops 100000000 | bytes 700000 | tf_op jit(solution)/shard_map/example_terms/pallas_call | solution.py:251
  20.5 0.1 collective-permute-start
  20.6 1.2 %collective-permute-done = f32[64,256]{1,0:T(8,128)S(1)} collective-permute-done((f32[64,256]{1,0:T(8,128)S(1)}, f32[64,256]{1,0:T(8,128)S(1)}, u32[]{:S(2)}, u32[]{:S(2)}) %collective-permute-start) | collective-permute-done | bytes 65568 | tf_op jit(solution)/shard_map/ppermute | solution.py:313
  21.8 0.0 copy-start.2
  21.9 0.7 %broadcast_in_dim.2 = bf16[8,64,256]{2,1,0:T(8,128)(2,1)} broadcast(bf16[64,256]{1,0:T(8,128)(2,1)S(1)} %add_convert_fusion._after), dimensions={1,2} | broadcast | bytes 294912 | tf_op jit(solution)/shard_map/broadcast_in_dim | solution.py:315
  22.6 8.6 %all-to-all-start.1 = ((bf16[8,64,256]{2,1,0:T(8,128)(2,1)}), bf16[8,64,256]{2,1,0:T(8,128)(2,1)S(1)}, u32[]{:S(2)}, u32[]{:S(2)}) async-start(bf16[8,64,256]{2,1,0:T(8,128)(2,1)} %broadcast_in_dim.2), calls=%async_computation.1 | async-start | bytes 524288 | tf_op jit(solution)/shard_map/all_to_all | solution.py:317
  31.1 0.0 copy-done.2
  31.1 0.0 copy-start
  31.1 13.2 %grads.1 = (bf16[688,1024]{1,0:T(8,128)(2,1)}, bf16[688,1024]{1,0:T(8,128)(2,1)}) custom-call(bf16[1024,4096]{1,0:T(8,128)(2,1)} %grad_ref.3, bf16[688,4096]{1,0:T(8,128)(2,1)} %weight_ref.1, bf16[688,1024]{1,0:T(8,128)(2,1)} %bitcast.9, bf16[688,1024]{1,0:T(8,128)(2,1)} %bitcast.11, bf16[64,256]{1,0:T(8,128)(2,1)} %copy-done.2), custom_call_target="tpu_custom_call" | custom-call | flops 5771362304 | bytes 19660800 | tf_op jit(solution)/shard_map/grads/pallas_call | solution.py:195
  44.4 0.0 all-to-all-done.1.terms_ref
  44.4 0.0 copy-done
  44.4 0.2 score_parts.1
  44.6 10.6 %all_to_all.16.parts_ref = f32[16,8,128]{2,1,0:T(8,128)S(1)} all-to-all(f32[16,8,128]{2,1,0:T(8,128)S(1)} %score_parts.1), channel_id=1, replica_groups=mesh['dp'=16,'tensor'=16] {'tensor'}, dimensions={0} | all-to-all | bytes 131072 | tf_op jit(solution)/shard_map/all_to_all | solution.py:322
  55.2 0.6 %final_sum.1 = f32[4,256]{1,0:T(4,128)} custom-call(f32[16,8,128]{2,1,0:T(8,128)S(1)} %all_to_all.16.parts_ref), custom_call_target="tpu_custom_call" | custom-call | flops 100000 | bytes 70000 | tf_op jit(solution)/shard_map/final_sum/pallas_call | solution.py:295
  (1 shorter events, 0.0 us)
Async XLA Ops:
  0.6 19.3 %copy-start.1 = (s32[1024]{0:T(1024)S(1)}, s32[1024]{0:T(1024)}, u32[]{:S(2)}) copy-start(s32[1024]{0:T(1024)} %param.14) | copy-start | bytes 12292
  20.5 1.3 %collective-permute-start = (f32[64,256]{1,0:T(8,128)S(1)}, f32[64,256]{1,0:T(8,128)S(1)}, u32[]{:S(2)}, u32[]{:S(2)}) collective-permute-start(f32[64,256]{1,0:T(8,128)S(1)} %example_terms.1), channel_id=1, source_target_pairs={{0,16},{16,0},{32,48},{48,32},{64,80},{80,64},{96,112},{112,96},{1... | collective-permute-start | bytes 196616 | tf_op jit(solution)/shard_map/ppermute | solution.py:313
  21.8 9.3 %copy-start.2 = (bf16[64,256]{1,0:T(8,128)(2,1)}, bf16[64,256]{1,0:T(8,128)(2,1)S(1)}, u32[]{:S(2)}) copy-start(bf16[64,256]{1,0:T(8,128)(2,1)S(1)} %add_convert_fusion._after) | copy-start | bytes 98308
  22.6 21.8 %all-to-all-start.1 = ((bf16[8,64,256]{2,1,0:T(8,128)(2,1)}), bf16[8,64,256]{2,1,0:T(8,128)(2,1)S(1)}, u32[]{:S(2)}, u32[]{:S(2)}) async-start(bf16[8,64,256]{2,1,0:T(8,128)(2,1)} %broadcast_in_dim.2), calls=%async_computation.1 | async-start | bytes 524288 | tf_op jit(solution)/shard_map/all_to_all | solution.py:317
  31.1 13.3 %copy-start = (bf16[256,256]{1,0:T(8,128)(2,1)S(1)}, bf16[256,256]{1,0:T(8,128)(2,1)}, u32[]{:S(2)}) copy-start(bf16[256,256]{1,0:T(8,128)(2,1)} %queries_ref.1) | copy-start | bytes 393220
